TPU v7x, 32 devices: a whole 2x2x4 slice. The times are simulated.
32 devices in a mesh: groups: 2 (over x), tm: 16 (over z, y, core).
Axes of the slice: x: 2, y: 2, z: 4, core: 2. Of those that a mesh axis runs over, the one named last changes fastest.
Arguments:
- spatial: float32 [256, 256], replicated, as said below
- persistence: float32 [64], P(('groups', 'tm')), parts along dimension 0, as said below
- obs_weight: float32 [64, 256], P(('groups', 'tm')), parts along dimension 0, as said below
- right_side: float32 [64, 256, 256], P(('groups', 'tm')), parts along dimension 0, as said below
Outputs:
- solution: float32 [64, 256, 256], P(('groups', 'tm')), parts along dimension 0
There are 2 independent parts, one for each index of `groups`. A program takes and returns all parts, laid end to end along the dimension named above; an argument that names none is the same for every part. Nothing has to cross between parts.
Inputs may be any that keep to these rules, and one draw needn't show every extreme that they name: spatial is symmetric and positive definite. `persistence`: every entry lies between 0.9 and 0.997. `obs_weight`: every entry lies between 0.00002 and 0.016. `right_side`: every entry lies between -0.012 and 0.012.
All inputs are finite; a program needn't handle non-finite values.
Results may differ from a plain program's by a relative error of at most 0.0003.
Values sent between devices are 32-bit elements; how exact they have to be, the bound alone decides.
No kernel may reach another device: no remote copies, remote signals or barrier semaphores. Data moves between devices by JAX's collectives and lax.ppermute only.
A program may use at most 128 MiB of HBM per device.

v0:
```python
import jax
import jax.numpy as jnp
from jax import lax
from jax.sharding import PartitionSpec as P

HIGH = lax.Precision.HIGHEST


def from_behind(value, axis, steps):
    count = lax.axis_size(axis)
    initial, last = (max(0, -steps), min(count, count - steps))
    return lax.ppermute(value, axis, [(source, source + steps) for source in range(initial, last)])


def product(left, right):
    return jnp.matmul(left, right, precision=HIGH)


def forward_solve(factor, values):
    return lax.linalg.triangular_solve(factor, values, left_side=True, lower=True)


def backward_solve(factor, values):
    return lax.linalg.triangular_solve(factor, values, left_side=True, lower=True, transpose_a=True)


def split_below(values, stride):
    return from_behind(values, "tm", stride)


def split_above(values, stride):
    return from_behind(values, "tm", -stride)


def factor_step(diagonal_block, lower_block, upper_link):
    factor = jnp.linalg.cholesky(diagonal_block)
    low_part = forward_solve(factor, lower_block)
    high_part = forward_solve(factor, upper_link.T)
    return (factor, low_part, high_part)


def coupling_terms(low_part, high_part):
    high_diag = product(high_part.T, high_part)
    high_link = -product(high_part.T, low_part)
    low_diag = product(low_part.T, low_part)
    return (high_diag, high_link, low_diag)


def reduce_matrices(operands):
    diagonal_block, lower_block, upper_link, kept_factor, kept_low, kept_high = operands
    factor, low_part, high_part = factor_step(diagonal_block, lower_block, upper_link)
    high_diag, high_link, low_diag = coupling_terms(low_part, high_part)
    return (factor, low_part, high_part, high_diag, high_link, low_diag)


def skip_matrices(operands):
    zeroed = jnp.zeros_like(operands[0])
    return (operands[3], operands[4], operands[5], zeroed, zeroed, zeroed)


def reduce_vector(operands):
    factor, low_part, high_part, vector, kept_solved = operands
    solved = forward_solve(factor, vector)
    return (solved, product(high_part.T, solved), product(low_part.T, solved))


def skip_vector(operands):
    zeroed = jnp.zeros_like(operands[3])
    return (operands[4], zeroed, zeroed)


def merge_blocks(operands):
    diagonal_block, lower_block, below_diag, above_diag, subdiagonal_matrix = operands
    return (diagonal_block - below_diag - above_diag, subdiagonal_matrix)


def keep_blocks(operands):
    return (operands[0], operands[1])


def merge_vector(operands):
    return operands[0] - operands[1] - operands[2]


def keep_vector(operands):
    return operands[0]


def factor_final(operands):
    return jnp.linalg.cholesky(operands[0])


def keep_factor(operands):
    return operands[1]


def back_step(operands):
    factor, low_part, high_part, solved, below, above, current = operands
    return backward_solve(factor, solved - product(low_part, below) - product(high_part, above))


def skip_back(operands):
    return operands[6]


def body(spatial, persistence, obs_weight, right_side):
    node_count = spatial.shape[0]
    column_count = right_side.shape[2]
    identity = jnp.eye(node_count, dtype=jnp.float32)
    devices_count = lax.axis_size("tm")
    tree_depth = devices_count.bit_length() - 1
    location_slot = lax.axis_index("tm")
    quadratic_matrix = jnp.zeros((node_count, node_count), jnp.float32)
    block = jnp.zeros((node_count, column_count), jnp.float32)
    first_block = (1.0 + persistence[0] * persistence[0]) * spatial + obs_weight[0][
        None, :
    ] * identity
    first_lower = jnp.where(location_slot > 0, -persistence[0], 0.0) * spatial
    retained_block = (1.0 + persistence[1] * persistence[1]) * spatial + obs_weight[1][
        None, :
    ] * identity
    kept_link = -persistence[1] * spatial
    first_factor, first_low, leading_high = factor_step(first_block, first_lower, kept_link)
    high_diag, high_link, low_diag = coupling_terms(first_low, leading_high)
    first_solved = forward_solve(first_factor, right_side[0])
    arrived = from_behind(low_diag, "tm", -1)
    vector = right_side[1]
    diagonal_block = retained_block - high_diag - arrived
    lower_block = high_link
    saved_factor = identity
    saved_low = quadratic_matrix
    saved_high = quadratic_matrix
    saved_solved = block
    for depth_index in range(tree_depth):
        stride = 1 << depth_index
        phase = (location_slot + 1) % (2 * stride)
        eliminated = phase == stride
        keeper = phase == 0
        upper_link = split_above(lower_block, stride)
        saved_factor, saved_low, saved_high, up_diag, up_link, down_diag = lax.cond(
            eliminated,
            reduce_matrices,
            skip_matrices,
            (diagonal_block, lower_block, upper_link, saved_factor, saved_low, saved_high),
        )
        below_diag, subdiagonal_matrix = split_below((up_diag, up_link), stride)
        above_diag = split_above(down_diag, stride)
        diagonal_block, lower_block = lax.cond(
            keeper,
            merge_blocks,
            keep_blocks,
            (diagonal_block, lower_block, below_diag, above_diag, subdiagonal_matrix),
        )
    final_device = location_slot == devices_count - 1
    saved_factor = lax.cond(final_device, factor_final, keep_factor, (diagonal_block, saved_factor))
    arrived_rhs = from_behind(product(first_low.T, first_solved), "tm", -1)
    vector = right_side[1] - product(leading_high.T, first_solved) - arrived_rhs
    for depth_index in range(tree_depth):
        stride = 1 << depth_index
        phase = (location_slot + 1) % (2 * stride)
        eliminated = phase == stride
        keeper = phase == 0
        saved_solved, up_rhs, down_rhs = lax.cond(
            eliminated,
            reduce_vector,
            skip_vector,
            (saved_factor, saved_low, saved_high, vector, saved_solved),
        )
        below_rhs = split_below(up_rhs, stride)
        above_rhs = split_above(down_rhs, stride)
        vector = lax.cond(keeper, merge_vector, keep_vector, (vector, below_rhs, above_rhs))
    saved_solved = lax.cond(
        final_device,
        reduce_vector,
        skip_vector,
        (saved_factor, saved_low, saved_high, vector, saved_solved),
    )[0]
    solution = lax.cond(
        final_device,
        back_step,
        skip_back,
        (saved_factor, saved_low, saved_high, saved_solved, block, block, block),
    )
    for depth_index in reversed(range(tree_depth)):
        stride = 1 << depth_index
        phase = (location_slot + 1) % (2 * stride)
        eliminated = phase == stride
        below = split_below(solution, stride)
        above = split_above(solution, stride)
        solution = lax.cond(
            eliminated,
            back_step,
            skip_back,
            (saved_factor, saved_low, saved_high, saved_solved, below, above, solution),
        )
    previous = from_behind(solution, "tm", 1)
    first_solution = backward_solve(
        first_factor, first_solved - product(first_low, previous) - product(leading_high, solution)
    )
    return jnp.stack([first_solution, solution])


def solution(mesh):
    placed = (P(), P(("groups", "tm")), P(("groups", "tm"), None), P(("groups", "tm"), None, None))
    return jax.shard_map(
        body, mesh=mesh, in_specs=placed, out_specs=P(("groups", "tm"), None, None), check_vma=False
    )
```

profile of v0, /device:TPU:1, one launch (start us, length us, event | category | flops | bytes accessed | tf_op | source)
XLA Modules:
  0.0 803.0 jit_solution(4528170887354542353)
XLA Ops:
  5.3 11.7 %cholesky.468 = f32[128,128]{1,0:T(8,128)S(1)} custom-call(f32[128,128]{1,0:T(8,128)S(1)} %cholesky.513), custom_call_target="Cholesky" | custom-call | tf_op jit(solution)/shard_map/jit(cholesky)/cholesky | solution.py:36
  17.1 9.8 %custom-call.62 = f32[1,128,128]{1,2,0:T(8,128)S(1)} custom-call(f32[1,128,128]{2,1,0:T(8,128)S(1)} %get-tuple-element.841), custom_call_target="InvertDiagBlocksLowerTriangular" | custom-call | tf_op jit(solution)/shard_map/jit(cholesky)/cholesky | solution.py:36
  27.4 11.7 %cholesky.485 = f32[128,128]{1,0:T(8,128)S(1)} custom-call(f32[128,128]{1,0:T(8,128)S(1)} %convolution_subtract_fusion.37), custom_call_target="Cholesky" | custom-call | tf_op jit(solution)/shard_map/jit(cholesky)/cholesky | solution.py:36
  41.2 4.2 while.58
  45.5 19.7 %custom-call.66 = f32[2,128,128]{1,2,0:T(8,128)S(1)} custom-call(f32[2,128,128]{2,1,0:T(8,128)S(1)} %get-tuple-element.617), custom_call_target="InvertDiagBlocksLowerTriangular" | custom-call | tf_op jit(solution)/shard_map/triangular_solve/custom-call.4 | solution.py:24
  66.7 2.0 collective-permute-start
  70.3 1.9 collective-permute-start.1
  73.6 1.7 collective-permute-done
  75.9 3.0 collective-permute-done.1
  78.9 9.7 %conditional.23 = (f32[256,256]{1,0:T(8,128)S(1)}, f32[256,256]{1,0:T(8,128)}, f32[256,256]{1,0:T(8,128)}, f32[256,256]{1,0:T(8,128)S(1)}, f32[256,256]{1,0:T(8,128)S(1)}, /*index=5*/f32[256,256]{1,0:T(8,128)S(1)}) conditional(s32[]{:T(128)} %convert_element_type.23, f32[256,256]{0,1:T(8,128)S(1)} %fusion.110, (f32[256,256]{0,1:T(8,128)S(1)}, ...), branch_computations={%region_4.7_spmd, %region_5.8_spmd} | conditional | flops 957104384 | bytes 8587519 | solution.py:140
  88.6 61.0 %collective-permute-start.2 = (f32[256,256]{1,0:T(8,128)S(1)}, f32[256,256]{1,0:T(8,128)S(1)}, u32[]{:S(2)}, u32[]{:S(2)}) collective-permute-start(f32[256,256]{1,0:T(8,128)S(1)} %get-tuple-element.411), channel_id=1, source_target_pairs={{0,1},{1,2},{2,3},{3,4},{4,5},{5,6},{6,7},{7,8},{8,9},{9,10},{10,1... | collective-permute-start | bytes 786440 | tf_op jit(solution)/shard_map/ppermute | solution.py:12
  149.5 1.9 collective-permute-start.3
  151.5 3.6 collective-permute-start.4
  155.1 2.1 collective-permute-done.3
  157.2 4.0 collective-permute-done.4
  162.8 7.7 collective-permute-done.5
  170.5 68.5 %conditional.25 = (f32[256,256]{1,0:T(8,128)S(1)}, f32[256,256]{1,0:T(8,128)}, f32[256,256]{1,0:T(8,128)}, f32[256,256]{1,0:T(8,128)S(1)}, f32[256,256]{1,0:T(8,128)S(1)}, /*index=5*/f32[256,256]{1,0:T(8,128)S(1)}) conditional(s32[]{:T(128)} %convert_element_type.24, (f32[256,256]{1,0:T(8,128)S(1)}, f32[256,256]{1,0:T(8,128)}, ...), branch_computations={%region_8.11_spmd, %region_9.12_spmd} | conditional | flops 957104384 | bytes 8587519 | solution.py:140
  170.7 11.7 %cholesky.332 = f32[128,128]{1,0:T(8,128)S(1)} custom-call(f32[128,128]{1,0:T(8,128)S(1)} %cholesky.504), custom_call_target="Cholesky" | custom-call | tf_op jit(solution)/shard_map/cond/branch_1_fun/jit(cholesky)/cholesky | solution.py:36
  182.5 9.8 %custom-call.42 = f32[1,128,128]{1,2,0:T(8,128)S(1)} custom-call(f32[1,128,128]{2,1,0:T(8,128)S(1)} %get-tuple-element.815), custom_call_target="InvertDiagBlocksLowerTriangular" | custom-call | tf_op jit(solution)/shard_map/cond/branch_1_fun/jit(cholesky)/cholesky | solution.py:36
  192.8 11.7 %cholesky.349 = f32[128,128]{1,0:T(8,128)S(1)} custom-call(f32[128,128]{1,0:T(8,128)S(1)} %convolution_subtract_fusion.7), custom_call_target="Cholesky" | custom-call | tf_op jit(solution)/shard_map/cond/branch_1_fun/jit(cholesky)/cholesky | solution.py:36
  206.6 4.3 while.45
  210.9 19.7 %custom-call.43 = f32[2,128,128]{1,2,0:T(8,128)S(1)} custom-call(f32[2,128,128]{2,1,0:T(8,128)S(1)} %get-tuple-element.598), custom_call_target="InvertDiagBlocksLowerTriangular" | custom-call | tf_op jit(solution)/shard_map/cond/branch_1_fun/triangular_solve/custom-call.0 | solution.py:20
  235.6 1.6 convolution_negate_fusion.1
  237.2 1.7 fusion.161
  241.7 5.7 collective-permute-start.8
  247.4 1.8 collective-permute-done.7
  249.2 3.3 collective-permute-done.8
  254.3 6.2 collective-permute-done.9
  260.5 10.7 %conditional.27 = (f32[256,256]{1,0:T(8,128)S(1)}, f32[256,256]{1,0:T(8,128)}, f32[256,256]{1,0:T(8,128)}, f32[256,256]{1,0:T(8,128)}, f32[256,256]{1,0:T(8,128)}, /*index=5*/f32[256,256]{1,0:T(8,128)}) conditional(s32[]{:T(128)} %convert_element_type.25, (f32[256,256]{1,0:T(8,128)S(1)}, f32[256,256]{1,0:T(8,128)}, ...), branch_computations={%region_12.15_spmd, %region_13.16_spmd} | conditional | flops 957104384 | bytes 8587519 | solution.py:140
  271.2 3.4 collective-permute-start.10
  275.9 4.0 collective-permute-start.12
  285.4 1.9 collective-permute-start.16
  287.3 7.0 collective-permute-done.13
  294.3 9.7 %conditional.29 = (f32[256,256]{1,0:T(8,128)S(1)}, f32[256,256]{1,0:T(8,128)}, f32[256,256]{1,0:T(8,128)}, f32[256,256]{1,0:T(8,128)}, f32[256,256]{1,0:T(8,128)}) conditional(s32[]{:T(128)} %convert_element_type.50, (f32[256,256]{1,0:T(8,128)S(1)}, f32[256,256]{1,0:T(8,128)}, f32[256,256]{1,0:T(8,128)}) %tuple.191, (f32[256,256]{1,0:T(8,128)S(1)}, ...), branch_computations={%region_16.19_spmd, %region_17.20_spmd} | conditional | flops 755712256 | bytes 9898287 | solution.py:140
  307.4 1.7 collective-permute-done.14
  309.2 6.1 collective-permute-done.15
  316.4 62.9 %collective-permute-start.17 = (f32[256,256]{1,0:T(8,128)S(1)}, f32[256,256]{1,0:T(8,128)S(1)}, u32[]{:S(2)}, u32[]{:S(2)}) collective-permute-start(f32[256,256]{1,0:T(8,128)S(1)} %copy.23), channel_id=1, source_target_pairs={{0,1},{1,2},{2,3},{3,4},{4,5},{5,6},{6,7},{7,8},{8,9},{9,10},{10,1... | collective-permute-start | bytes 786440 | tf_op jit(solution)/shard_map/ppermute | solution.py:12
  379.5 27.3 %collective-permute-start.18 = (f32[256,256]{1,0:T(8,128)S(1)}, f32[256,256]{1,0:T(8,128)S(1)}, u32[]{:S(2)}, u32[]{:S(2)}) collective-permute-start(f32[256,256]{1,0:T(8,128)S(1)} %copy.24), channel_id=1, source_target_pairs={{1,0},{2,1},{3,2},{4,3},{5,4},{6,5},{7,6},{8,7},{9,8},{10,9},{11,1... | collective-permute-start | bytes 786440 | tf_op jit(solution)/shard_map/ppermute | solution.py:12
  408.1 28.6 %conditional.34 = (f32[256,256]{1,0:T(8,128)}, f32[256,256]{0,1:T(8,128)S(1)}, f32[256,256]{0,1:T(8,128)S(1)}) conditional(s32[]{:T(128)} %convert_element_type.24, f32[256,256]{1,0:T(8,128)} %get-tuple-element.438, (f32[256,256]{1,0:T(8,128)S(1)}, f32[256,256]{1,0:T(8,128)S(1)}, f32[256,256]{1,0:T(8,128)}, f32[256,256]{1,0:T(8,128)}) %tuple.198), branch_computations={%region_26.29_spmd, %region_27.30_spmd} | conditional | flops 553877504 | bytes 3866845 | solution.py:163
  408.3 3.9 while.49
  412.2 19.7 %custom-call.53 = f32[2,128,128]{1,2,0:T(8,128)S(1)} custom-call(f32[2,128,128]{2,1,0:T(8,128)S(1)} %get-tuple-element.605), custom_call_target="InvertDiagBlocksLowerTriangular" | custom-call | tf_op jit(solution)/shard_map/cond/branch_1_fun/triangular_solve/custom-call.0 | solution.py:20
  439.6 1.8 collective-permute-done.19
  441.5 38.2 %collective-permute-done.20 = f32[256,256]{1,0:T(8,128)S(1)} collective-permute-done((f32[256,256]{1,0:T(8,128)S(1)}, f32[256,256]{1,0:T(8,128)S(1)}, u32[]{:S(2)}, u32[]{:S(2)}) %collective-permute-start.20) | collective-permute-done | bytes 262176 | tf_op jit(solution)/shard_map/ppermute | solution.py:12
  480.3 3.8 collective-permute-start.21
  485.6 1.8 collective-permute-done.21
  487.4 39.5 %collective-permute-done.22 = f32[256,256]{1,0:T(8,128)S(1)} collective-permute-done((f32[256,256]{1,0:T(8,128)S(1)}, f32[256,256]{1,0:T(8,128)S(1)}, u32[]{:S(2)}, u32[]{:S(2)}) %collective-permute-start.22) | collective-permute-done | bytes 262176 | tf_op jit(solution)/shard_map/ppermute | solution.py:12
  527.1 2.6 collective-permute-start.23
  531.1 3.2 collective-permute-done.23
  534.3 7.0 collective-permute-done.24
  544.4 2.0 collective-permute-done.25
  546.4 9.4 %collective-permute-done.26 = f32[256,256]{1,0:T(8,128)S(1)} collective-permute-done((f32[256,256]{1,0:T(8,128)S(1)}, f32[256,256]{1,0:T(8,128)S(1)}, u32[]{:S(2)}, u32[]{:S(2)}) %collective-permute-start.26) | collective-permute-done | bytes 262176 | tf_op jit(solution)/shard_map/ppermute | solution.py:12
  558.4 2.0 collective-permute-done.27
  560.4 3.8 collective-permute-done.28
  564.5 158.6 %collective-permute-start.29 = (f32[256,256]{1,0:T(8,128)S(1)}, f32[256,256]{1,0:T(8,128)S(1)}, u32[]{:S(2)}, u32[]{:S(2)}) collective-permute-start(f32[256,256]{1,0:T(8,128)S(1)} %get-tuple-element.1603), channel_id=1, source_target_pairs={{0,2},{1,3},{2,4},{3,5},{4,6},{5,7},{6,8},{7,9},{8,10},{9,11},{10,... | collective-permute-start | bytes 786440 | tf_op jit(solution)/shard_map/ppermute | solution.py:12
  724.4 2.0 collective-permute-done.29
  726.4 3.8 collective-permute-done.30
  730.2 27.3 %conditional.44 = (f32[256,256]{1,0:T(8,128)S(1)}) conditional(s32[]{:T(128)} %convert_element_type.24, f32[256,256]{1,0:T(8,128)S(1)} %get-tuple-element.1603, (f32[256,256]{1,0:T(8,128)}, f32[256,256]{1,0:T(8,128)S(1)}, f32[256,256]{1,0:T(8,128)}, f32[256,256]{1,0:T(8,128)}, f32[256,256]{1,0:T(8,128)S(1)}, ...), branch_computations={%region_48.52_spmd, %region_49.53_spmd} | conditional | flops 554008576 | bytes 4391117 | solution.py:190
  733.1 3.9 while.56
  737.0 19.7 %custom-call.60 = f32[2,128,128]{1,2,0:T(8,128)S(1)} custom-call(f32[2,128,128]{2,1,0:T(8,128)S(1)} %get-tuple-element.612), custom_call_target="InvertDiagBlocksLowerTriangular" | custom-call | tf_op jit(solution)/shard_map/cond/branch_1_fun/triangular_solve/custom-call.4 | solution.py:24
  757.6 1.9 collective-permute-start.31
  759.5 2.4 collective-permute-start.32
  761.9 3.7 collective-permute-done.31
  767.2 30.2 %collective-permute-start.33 = (f32[256,256]{1,0:T(8,128)S(1)}, f32[256,256]{1,0:T(8,128)S(1)}, u32[]{:S(2)}, u32[]{:S(2)}) collective-permute-start(f32[256,256]{1,0:T(8,128)S(1)} %get-tuple-element.1605), channel_id=1, source_target_pairs={{0,1},{1,2},{2,3},{3,4},{4,5},{5,6},{6,7},{7,8},{8,9},{9,10},{10,1... | collective-permute-start | bytes 786440 | tf_op jit(solution)/shard_map/ppermute | solution.py:12
  797.7 2.9 collective-permute-done.33
  (189 shorter events, 81.0 us)
Async XLA Ops:
  0.0 0.7 copy-start.5
  3.8 1.1 copy-start.4
  41.1 24.0 %copy-start = (f32[256,256]{1,0:T(8,128)S(1)}, f32[256,256]{1,0:T(8,128)}, u32[]{:S(2)}) copy-start(f32[256,256]{1,0:T(8,128)} %param.55) | copy-start | bytes 786436
  66.7 8.6 %collective-permute-start = (f32[256,256]{0,1:T(8,128)S(1)}, f32[256,256]{0,1:T(8,128)S(1)}, u32[]{:S(2)}, u32[]{:S(2)}) collective-permute-start(f32[256,256]{0,1:T(8,128)S(1)} %fusion.122), channel_id=1, source_target_pairs={{1,0},{2,1},{3,2},{4,3},{5,4},{6,5},{7,6},{8,7},{9,8},{10,9},{11,1... | collective-permute-start | bytes 786440 | tf_op jit(solution)/shard_map/ppermute | solution.py:12
  70.3 8.5 %collective-permute-start.1 = (f32[256,256]{1,0:T(8,128)S(1)}, f32[256,256]{1,0:T(8,128)S(1)}, u32[]{:S(2)}, u32[]{:S(2)}) collective-permute-start(f32[256,256]{1,0:T(8,128)S(1)} %convolution_negate_fusion.3), channel_id=1, source_target_pairs={{1,0},{2,1},{3,2},{4,3},{5,4},{6,5},{7,6},{8,7},{9,8},{10,9},{11,1... | collective-permute-start | bytes 786440 | tf_op jit(solution)/shard_map/ppermute | solution.py:12
  88.6 66.5 %collective-permute-start.2 = (f32[256,256]{1,0:T(8,128)S(1)}, f32[256,256]{1,0:T(8,128)S(1)}, u32[]{:S(2)}, u32[]{:S(2)}) collective-permute-start(f32[256,256]{1,0:T(8,128)S(1)} %get-tuple-element.411), channel_id=1, source_target_pairs={{0,1},{1,2},{2,3},{3,4},{4,5},{5,6},{6,7},{7,8},{8,9},{9,10},{10,1... | collective-permute-start | bytes 786440 | tf_op jit(solution)/shard_map/ppermute | solution.py:12
  149.5 7.7 collective-permute-start.3
  151.5 9.8 %collective-permute-start.4 = (f32[256,256]{1,0:T(8,128)S(1)}, f32[256,256]{1,0:T(8,128)S(1)}, u32[]{:S(2)}, u32[]{:S(2)}) collective-permute-start(f32[256,256]{1,0:T(8,128)S(1)} %get-tuple-element.413), channel_id=1, source_target_pairs={{0,1},{1,2},{2,3},{3,4},{4,5},{5,6},{6,7},{7,8},{8,9},{9,10},{10,1... | collective-permute-start | bytes 786440 | tf_op jit(solution)/shard_map/ppermute | solution.py:12
  161.5 9.0 %collective-permute-start.5 = (f32[256,256]{1,0:T(8,128)S(1)}, f32[256,256]{1,0:T(8,128)S(1)}, u32[]{:S(2)}, u32[]{:S(2)}) collective-permute-start(f32[256,256]{1,0:T(8,128)S(1)} %get-tuple-element.415), channel_id=1, source_target_pairs={{2,0},{3,1},{4,2},{5,3},{6,4},{7,5},{8,6},{9,7},{10,8},{11,9},{12,... | collective-permute-start | bytes 786440 | tf_op jit(solution)/shard_map/ppermute | solution.py:12
  239.1 8.3 %collective-permute-start.6 = (f32[256,256]{1,0:T(8,128)S(1)}, f32[256,256]{1,0:T(8,128)S(1)}, u32[]{:S(2)}, u32[]{:S(2)}) collective-permute-start(f32[256,256]{1,0:T(8,128)S(1)} %get-tuple-element.419), channel_id=1, source_target_pairs={{0,2},{1,3},{2,4},{3,5},{4,6},{5,7},{6,8},{7,9},{8,10},{9,11},{10,... | collective-permute-start | bytes 786440 | tf_op jit(solution)/shard_map/ppermute | solution.py:12
  240.4 8.8 %collective-permute-start.7 = (f32[256,256]{1,0:T(8,128)S(1)}, f32[256,256]{1,0:T(8,128)S(1)}, u32[]{:S(2)}, u32[]{:S(2)}) collective-permute-start(f32[256,256]{1,0:T(8,128)S(1)} %get-tuple-element.420), channel_id=1, source_target_pairs={{2,0},{3,1},{4,2},{5,3},{6,4},{7,5},{8,6},{9,7},{10,8},{11,9},{12,... | collective-permute-start | bytes 786440 | tf_op jit(solution)/shard_map/ppermute | solution.py:12
  241.7 10.8 %collective-permute-start.8 = (f32[256,256]{1,0:T(8,128)S(1)}, f32[256,256]{1,0:T(8,128)S(1)}, u32[]{:S(2)}, u32[]{:S(2)}) collective-permute-start(f32[256,256]{1,0:T(8,128)S(1)} %get-tuple-element.421), channel_id=1, source_target_pairs={{0,2},{1,3},{2,4},{3,5},{4,6},{5,7},{6,8},{7,9},{8,10},{9,11},{10,... | collective-permute-start | bytes 786440 | tf_op jit(solution)/shard_map/ppermute | solution.py:12
  252.5 1.4 copy-start.1
  252.5 8.0 collective-permute-start.9
  271.2 9.3 %collective-permute-start.10 = (f32[256,256]{1,0:T(8,128)}, f32[256,256]{1,0:T(8,128)S(1)}, u32[]{:S(2)}, u32[]{:S(2)}) collective-permute-start(f32[256,256]{1,0:T(8,128)} %get-tuple-element.427), channel_id=1, source_target_pairs={{0,4},{1,5},{2,6},{3,7},{4,8},{5,9},{6,10},{7,11},{8,12},{9,13},{1... | collective-permute-start | bytes 786440 | tf_op jit(solution)/shard_map/ppermute | solution.py:12
  274.6 7.4 collective-permute-start.11
  275.9 7.6 collective-permute-start.12
  283.5 10.8 %collective-permute-start.13 = (f32[256,256]{1,0:T(8,128)S(1)}, f32[256,256]{1,0:T(8,128)S(1)}, u32[]{:S(2)}, u32[]{:S(2)}) collective-permute-start(f32[256,256]{1,0:T(8,128)S(1)} %get-tuple-element.431), channel_id=1, source_target_pairs={{8,0},{9,1},{10,2},{11,3},{12,4},{13,5},{14,6},{15,7},{24,16},{25,... | collective-permute-start | bytes 786440 | tf_op jit(solution)/shard_map/ppermute | solution.py:12
  285.4 21.5 %collective-permute-start.16 = (f32[256,256]{1,0:T(8,128)S(1)}, f32[256,256]{1,0:T(8,128)S(1)}, u32[]{:S(2)}, u32[]{:S(2)}) collective-permute-start(f32[256,256]{1,0:T(8,128)S(1)} %fusion.111), channel_id=1, source_target_pairs={{1,0},{2,1},{3,2},{4,3},{5,4},{6,5},{7,6},{8,7},{9,8},{10,9},{11,1... | collective-permute-start | bytes 786440 | tf_op jit(solution)/shard_map/ppermute | solution.py:12
  304.0 5.1 collective-permute-start.14
  305.5 9.8 %collective-permute-start.15 = (f32[256,256]{1,0:T(8,128)}, f32[256,256]{1,0:T(8,128)S(1)}, u32[]{:S(2)}, u32[]{:S(2)}) collective-permute-start(f32[256,256]{1,0:T(8,128)} %get-tuple-element.436), channel_id=1, source_target_pairs={{8,0},{9,1},{10,2},{11,3},{12,4},{13,5},{14,6},{15,7},{24,16},{25,... | collective-permute-start | bytes 786440 | tf_op jit(solution)/shard_map/ppermute | solution.py:12
  316.4 90.4 %collective-permute-start.17 = (f32[256,256]{1,0:T(8,128)S(1)}, f32[256,256]{1,0:T(8,128)S(1)}, u32[]{:S(2)}, u32[]{:S(2)}) collective-permute-start(f32[256,256]{1,0:T(8,128)S(1)} %copy.23), channel_id=1, source_target_pairs={{0,1},{1,2},{2,3},{3,4},{4,5},{5,6},{6,7},{7,8},{8,9},{9,10},{10,1... | collective-permute-start | bytes 786440 | tf_op jit(solution)/shard_map/ppermute | solution.py:12
  379.5 28.5 %collective-permute-start.18 = (f32[256,256]{1,0:T(8,128)S(1)}, f32[256,256]{1,0:T(8,128)S(1)}, u32[]{:S(2)}, u32[]{:S(2)}) collective-permute-start(f32[256,256]{1,0:T(8,128)S(1)} %copy.24), channel_id=1, source_target_pairs={{1,0},{2,1},{3,2},{4,3},{5,4},{6,5},{7,6},{8,7},{9,8},{10,9},{11,1... | collective-permute-start | bytes 786440 | tf_op jit(solution)/shard_map/ppermute | solution.py:12
  436.9 4.6 collective-permute-start.19
  438.3 41.3 %collective-permute-start.20 = (f32[256,256]{1,0:T(8,128)S(1)}, f32[256,256]{1,0:T(8,128)S(1)}, u32[]{:S(2)}, u32[]{:S(2)}) collective-permute-start(f32[256,256]{1,0:T(8,128)S(1)} %copy.26), channel_id=1, source_target_pairs={{2,0},{3,1},{4,2},{5,3},{6,4},{7,5},{8,6},{9,7},{10,8},{11,9},{12,... | collective-permute-start | bytes 786440 | tf_op jit(solution)/shard_map/ppermute | solution.py:12
  480.3 7.1 collective-permute-start.21
  484.3 42.7 %collective-permute-start.22 = (f32[256,256]{1,0:T(8,128)S(1)}, f32[256,256]{1,0:T(8,128)S(1)}, u32[]{:S(2)}, u32[]{:S(2)}) collective-permute-start(f32[256,256]{1,0:T(8,128)S(1)} %copy.28), channel_id=1, source_target_pairs={{4,0},{5,1},{6,2},{7,3},{8,4},{9,5},{10,6},{11,7},{12,8},{13,9},{1... | collective-permute-start | bytes 786440 | tf_op jit(solution)/shard_map/ppermute | solution.py:12
  527.1 7.2 collective-permute-start.23
  529.8 11.5 %collective-permute-start.24 = (f32[256,256]{1,0:T(8,128)S(1)}, f32[256,256]{1,0:T(8,128)S(1)}, u32[]{:S(2)}, u32[]{:S(2)}) collective-permute-start(f32[256,256]{1,0:T(8,128)S(1)} %copy.30), channel_id=1, source_target_pairs={{8,0},{9,1},{10,2},{11,3},{12,4},{13,5},{14,6},{15,7},{24,16},{25,... | collective-permute-start | bytes 786440 | tf_op jit(solution)/shard_map/ppermute | solution.py:12
  541.6 4.8 collective-permute-start.25
  543.1 12.8 %collective-permute-start.26 = (f32[256,256]{1,0:T(8,128)S(1)}, f32[256,256]{1,0:T(8,128)S(1)}, u32[]{:S(2)}, u32[]{:S(2)}) collective-permute-start(f32[256,256]{1,0:T(8,128)S(1)} %get-tuple-element.1601), channel_id=1, source_target_pairs={{8,0},{9,1},{10,2},{11,3},{12,4},{13,5},{14,6},{15,7},{24,16},{25,... | collective-permute-start | bytes 786440 | tf_op jit(solution)/shard_map/ppermute | solution.py:12
  555.8 4.6 collective-permute-start.27
  557.1 7.1 collective-permute-start.28
  564.5 161.9 %collective-permute-start.29 = (f32[256,256]{1,0:T(8,128)S(1)}, f32[256,256]{1,0:T(8,128)S(1)}, u32[]{:S(2)}, u32[]{:S(2)}) collective-permute-start(f32[256,256]{1,0:T(8,128)S(1)} %get-tuple-element.1603), channel_id=1, source_target_pairs={{0,2},{1,3},{2,4},{3,5},{4,6},{5,7},{6,8},{7,9},{8,10},{9,11},{10,... | collective-permute-start | bytes 786440 | tf_op jit(solution)/shard_map/ppermute | solution.py:12
  723.1 7.1 collective-permute-start.30
  757.6 8.0 %collective-permute-start.31 = (f32[256,256]{1,0:T(8,128)S(1)}, f32[256,256]{1,0:T(8,128)S(1)}, u32[]{:S(2)}, u32[]{:S(2)}) collective-permute-start(f32[256,256]{1,0:T(8,128)S(1)} %get-tuple-element.1604), channel_id=1, source_target_pairs={{0,1},{1,2},{2,3},{3,4},{4,5},{5,6},{6,7},{7,8},{8,9},{9,10},{10,1... | collective-permute-start | bytes 786440 | tf_op jit(solution)/shard_map/ppermute | solution.py:12
  759.5 7.7 collective-permute-start.32
  767.2 33.5 %collective-permute-start.33 = (f32[256,256]{1,0:T(8,128)S(1)}, f32[256,256]{1,0:T(8,128)S(1)}, u32[]{:S(2)}, u32[]{:S(2)}) collective-permute-start(f32[256,256]{1,0:T(8,128)S(1)} %get-tuple-element.1605), channel_id=1, source_target_pairs={{0,1},{1,2},{2,3},{3,4},{4,5},{5,6},{6,7},{7,8},{8,9},{9,10},{10,1... | collective-permute-start | bytes 786440 | tf_op jit(solution)/shard_map/ppermute | solution.py:12
where the time goes:
time: 812 us; the launch traced here: 803 us
  starting transfers between devices  398 us (49%)
  waiting for transfers between devices  172 us (21%)
  other arithmetic  150 us (18%)
  loops' own time  28.4 us (3%)
  local copies, waits for them, and re-layouts  25.8 us (3%)
  matrix products  22.8 us (3%)
    ppermute x34, starting transfers between devices, from_behind(): lax.ppermute(value, axis, [(source, source + steps) for source in range(i...  398 us
    ppermute x34, waiting for transfers between devices, from_behind(): lax.ppermute(value, axis, [(source, source + steps) for source in range(i...  172 us
    another operation x12, other arithmetic, factor_step(): factor = jnp.linalg.cholesky(diagonal_block)  68 us
    another operation x11, other arithmetic, forward_solve(): lax.linalg.triangular_solve(factor, values, left_side=True, lower=True)  41.6 us
    another operation x9, other arithmetic, backward_solve(): lax.linalg.triangular_solve(factor, values, left_side=True, lower=True, t...  39.4 us
    another operation x4, loops' own time, body(): lax.cond(eliminated, reduce_matrices, skip_matrices, (diagonal_block, low...  26.5 us
  transfers between devices with their start and end apart: 34, of which 29 were waited for; matrix products, arithmetic and copies ran while one was open for 1% of the time, Pallas kernels for 0%

commit v1 on v0

v1 whole, which is shorter than its diff:
```python
import functools

import jax
import jax.numpy as jnp
from jax import lax
from jax.experimental import pallas as pl
from jax.experimental.pallas import tpu as pltpu
from jax.sharding import PartitionSpec as P

F32 = jnp.float32
BF16 = jnp.bfloat16
SUBLANES = 8
ENERGY_TOLERANCE = 1e-12
STEP_LIMIT = 2000
COARSE_LIMIT = 14
FINE_LIMIT = 80


def split(value):
    high = value.astype(BF16)
    return high, (value - high.astype(F32)).astype(BF16)


def dot(left, right):
    return jnp.dot(left, right, preferred_element_type=F32)


def split_dot(left, right_high, right_low):
    high, low = split(left)
    return dot(high, right_high) + dot(low, right_high) + dot(high, right_low)


def exact_dot(left, right):
    return jnp.dot(left, right, preferred_element_type=F32, precision=lax.Precision.HIGHEST)


def loop(count, body, start):
    if count <= 32:
        carry = start
        for i in range(count):
            carry = body(i, carry)
        return carry
    return lax.fori_loop(0, count, body, start)


def eye(size):
    rows = lax.broadcasted_iota(jnp.int32, (size, size), 0)
    columns = lax.broadcasted_iota(jnp.int32, (size, size), 1)
    return jnp.where(rows == columns, 1.0, 0.0).astype(F32)


def row_sum_norm(value):
    return jnp.max(jnp.sum(jnp.abs(value), axis=0, keepdims=True))


def invert(spatial, inverse):
    size = spatial.shape[0]
    identity = eye(size)
    high = spatial.astype(BF16)
    square = dot(high, high)
    bound = jnp.sqrt(row_sum_norm(square)) * 1.02
    scale = 1.9 / bound
    start = scale * (2.0 * identity - scale * spatial)
    inverse[...] = start

    def coarse_step(state):
        count, unused = state
        guess = inverse[...]
        residual = identity - dot(high, guess.astype(BF16))
        inverse[...] = guess + dot(guess.astype(BF16), residual.astype(BF16))
        return count + 1, row_sum_norm(residual)

    def coarse_goes_on(state):
        count, error = state
        return jnp.logical_and(count < COARSE_LIMIT, error > 0.3)

    unused, error = lax.while_loop(coarse_goes_on, coarse_step, (0, F32(1e30)))

    @pl.when(jnp.logical_not(error <= 0.3))
    def restart():
        inverse[...] = start

    def fine_step(state):
        count, unused = state
        guess = inverse[...]
        residual = identity - exact_dot(spatial, guess)
        inverse[...] = guess + exact_dot(guess, residual)
        return count + 1, row_sum_norm(residual)

    def fine_goes_on(state):
        count, error = state
        return jnp.logical_and(count < FINE_LIMIT, error > 0.3)

    lax.while_loop(fine_goes_on, fine_step, (0, F32(1e30)))
    result = inverse[...]
    inverse[...] = 0.5 * (result + result.T)


def solve_kernel(
    segments, per_segment, columns,
    received, spatial, out,
    x, r, p, h, z, q, w, e, d, inverse, s_high, s_low, g_high, g_low,
):
    size = spatial.shape[0]
    steps = segments * per_segment
    block = per_segment * columns

    def at(t):
        if isinstance(t, int):
            return pl.ds(t * columns, columns)
        return pl.ds(pl.multiple_of(t * columns, SUBLANES), columns)

    def source(t):
        if isinstance(t, int):
            return t // per_segment, t % per_segment
        return lax.div(t, per_segment), lax.rem(t, per_segment)

    def right_side(t):
        i, j = source(t)
        if isinstance(t, int):
            return received[i, pl.ds(j * columns, columns), :]
        return received[i, pl.ds(pl.multiple_of(j * columns, SUBLANES), columns), :]

    invert(spatial[...], inverse)
    s_high[...], s_low[...] = split(spatial[...])
    g_high[...], g_low[...] = split(inverse[...])

    def factor(t, last):
        i, j = source(t)
        weight = received[i, pl.ds(block + j, 1), :]
        rate = received[i, pl.ds(block + per_segment + j, 1), :]
        link = rate * last
        inverse_pivot = 1.0 / (1.0 + rate * rate - rate * link)
        w[t] = weight
        e[t] = link
        d[t] = inverse_pivot
        return inverse_pivot

    loop(steps, factor, jnp.zeros((1, size), F32))

    def over_lanes(value):
        return jnp.sum(value, axis=1, keepdims=True)

    def zero():
        return jnp.zeros((columns, size), F32)

    biggest = loop(steps, lambda t, acc: jnp.maximum(acc, jnp.abs(right_side(t))), zero())
    biggest = jnp.max(biggest, axis=1, keepdims=True)
    biggest = jnp.where(biggest > 0.0, biggest, 1.0)
    shrink = 1.0 / biggest

    def load(t, carry):
        r[at(t), :] = right_side(t) * shrink
        x[at(t), :] = zero()
        return carry

    loop(steps, load, 0)

    def precondition():
        z[...] = split_dot(r[...], g_high[...], g_low[...])

    def sweep():
        def down(t, last):
            value = z[at(t), :] + e[t] * last
            z[at(t), :] = value
            return value

        def up(k, carry):
            above, acc = carry
            t = steps - 1 - k
            value = z[at(t), :] * d[t] + above
            z[at(t), :] = value
            return e[t] * value, acc + r[at(t), :] * value

        loop(steps, down, zero())
        unused, acc = loop(steps, up, (zero(), zero()))
        return over_lanes(acc)

    precondition()
    h[...] = z[...]
    energy = sweep()
    p[...] = z[...]
    limit = energy * ENERGY_TOLERANCE

    def goes_on(state):
        count, unused, excess = state
        return jnp.logical_and(count < STEP_LIMIT, excess > 0.0)

    def step(state):
        count, energy, unused = state
        z[...] = split_dot(h[...], s_high[...], s_low[...])

        def curve(t, acc):
            direction = p[at(t), :]
            value = z[at(t), :] + w[t] * direction
            z[at(t), :] = value
            return acc + direction * value

        curvature = over_lanes(loop(steps, curve, zero()))
        alpha = jnp.where(curvature > 0.0, energy / jnp.where(curvature > 0.0, curvature, 1.0), 0.0)

        def advance(t, carry):
            x[at(t), :] += alpha * p[at(t), :]
            r[at(t), :] -= alpha * z[at(t), :]
            return carry

        loop(steps, advance, 0)
        precondition()
        q[...] = z[...]
        new_energy = sweep()
        beta = jnp.where(energy > 0.0, new_energy / jnp.where(energy > 0.0, energy, 1.0), 0.0)

        def turn(t, carry):
            p[at(t), :] = z[at(t), :] + beta * p[at(t), :]
            h[at(t), :] = q[at(t), :] + beta * h[at(t), :]
            return carry

        loop(steps, turn, 0)
        return count + 1, new_energy, jnp.max(new_energy - limit)

    lax.while_loop(goes_on, step, (0, energy, jnp.max(energy)))

    def store(t, carry):
        i, j = source(t)
        if isinstance(t, int):
            rows = pl.ds(j * columns, columns)
        else:
            rows = pl.ds(pl.multiple_of(j * columns, SUBLANES), columns)
        out[i, rows, :] = x[at(t), :] * biggest
        return carry

    loop(steps, store, 0)


def solve(received, spatial, segments, per_segment, columns):
    size = spatial.shape[0]
    steps = segments * per_segment
    rows = steps * columns
    state = pltpu.VMEM((rows, size), F32)
    per_step = pltpu.VMEM((steps, 1, size), F32)
    matrix = pltpu.VMEM((size, size), BF16)
    return pl.pallas_call(
        functools.partial(solve_kernel, segments, per_segment, columns),
        out_shape=jax.ShapeDtypeStruct((segments, per_segment * columns, size), F32),
        in_specs=[pl.BlockSpec(memory_space=pltpu.VMEM)] * 2,
        out_specs=pl.BlockSpec(memory_space=pltpu.VMEM),
        scratch_shapes=[state] * 6 + [per_step] * 3 + [pltpu.VMEM((size, size), F32)] + [matrix] * 4,
        compiler_params=pltpu.CompilerParams(vmem_limit_bytes=40 * 2**20),
        name="solve",
    )(received, spatial)


def body(spatial, persistence, obs_weight, right_side):
    devices = lax.axis_size("tm")
    per_segment, size, column_count = right_side.shape
    columns = column_count // devices
    padded = -(-columns // SUBLANES) * SUBLANES

    parts = jnp.swapaxes(right_side, 1, 2).reshape(per_segment, devices, columns, size)
    parts = jnp.swapaxes(parts, 0, 1).reshape(devices, per_segment * columns, size)
    rates = jnp.broadcast_to(persistence[:, None], (per_segment, size))
    shared = jnp.concatenate([obs_weight, rates])
    fill = -(per_segment * columns + 2 * per_segment) % SUBLANES
    shared = jnp.pad(shared, ((0, fill), (0, 0)))
    shared = jnp.broadcast_to(shared[None], (devices,) + shared.shape)
    received = lax.all_to_all(jnp.concatenate([parts, shared], axis=1), "tm", 0, 0, tiled=True)
    if padded != columns:
        block = received[:, : per_segment * columns].reshape(devices, per_segment, columns, size)
        block = jnp.pad(block, ((0, 0), (0, 0), (0, padded - columns), (0, 0)))
        block = block.reshape(devices, per_segment * padded, size)
        received = jnp.concatenate([block, received[:, per_segment * columns :]], axis=1)
    solved = solve(received, spatial, devices, per_segment, padded)
    if padded != columns:
        solved = solved.reshape(devices, per_segment, padded, size)[:, :, :columns]
        solved = solved.reshape(devices, per_segment * columns, size)
    returned = lax.all_to_all(solved, "tm", 0, 0, tiled=True)
    returned = returned.reshape(devices, per_segment, columns, size)
    return jnp.transpose(returned, (1, 3, 0, 2)).reshape(per_segment, size, column_count)


def solution(mesh):
    placed = (P(), P(("groups", "tm")), P(("groups", "tm"), None), P(("groups", "tm"), None, None))
    return jax.shard_map(
        body, mesh=mesh, in_specs=placed, out_specs=P(("groups", "tm"), None, None), check_vma=False
    )
```

time: 812 us -> 57.5 us (0.07)
  the two profiles are of different devices: /device:TPU:1 before, /device:TPU:0 now
where the time goes in v1:
time: 57.5 us; the launch traced here: 56.4 us
  blocking collectives  43.1 us (75%)
  Pallas kernels  10.1 us (18%)
  local copies, waits for them, and re-layouts  3 us (5%)
    all_to_all x1, blocking collectives, body(): lax.all_to_all(jnp.concatenate([parts, shared], axis=1), 'tm', 0, 0, tile...  25.6 us
    all_to_all x1, blocking collectives, body(): returned = lax.all_to_all(solved, 'tm', 0, 0, tiled=True)  17.5 us
    pallas_call x1, Pallas kernels, solve(): pl.pallas_call(functools.partial(solve_kernel, segments, per_segment, col...  10.1 us
    unnamed x7, local copies, waits for them, and re-layouts  1.84 us

profile of v1, /device:TPU:0, one launch (start us, length us, event | category | flops | bytes accessed | tf_op | source)
XLA Modules:
  0.0 56.4 jit_solution(4786639067640803185)
XLA Ops:
  0.0 1.2 %copy.7 = f32[2,256,256]{1,2,0:T(8,128)S(1)} copy(f32[2,256,256]{2,1,0:T(8,128)} %param.7) | data formatting | bytes 1048576 | tf_op args[3]
  1.2 0.0 copy-start.2
  1.3 0.0 copy-start.1
  1.3 0.6 %copy-done.2 = f32[2]{0:T(128)S(1)} copy-done((f32[2]{0:T(128)S(1)}, f32[2]{0:T(128)}, u32[]{:S(2)}) %copy-start.2) | copy-done | bytes 32
  1.9 0.1 pad.8.clone
  2.0 0.0 copy-done.1
  2.0 0.1 pad_maximum_fusion.1
  2.1 0.1 pad_maximum_fusion
  2.1 0.0 copy-start
  2.1 25.6 %all_to_all.10.received = f32[16,40,256]{2,1,0:T(8,128)S(1)} all-to-all(f32[16,40,256]{2,1,0:T(8,128)S(1)} %pad_maximum_fusion), channel_id=1, replica_groups=mesh['groups'=2,'tm'=16] {'tm'}, dimensions={0} | all-to-all | bytes 1310720 | tf_op jit(solution)/shard_map/all_to_all | solution.py:266
  27.7 0.0 copy-done
  27.7 10.1 %solve.1 = f32[16,32,256]{2,1,0:T(8,128)S(1)} custom-call(f32[16,40,256]{2,1,0:T(8,128)S(1)} %all_to_all.10.received, f32[256,256]{1,0:T(8,128)S(1)} %copy-done), custom_call_target="tpu_custom_call" | custom-call | tf_op jit(solution)/shard_map/solve/pallas_call | solution.py:242
  37.8 17.5 %all_to_all.11 = f32[16,32,256]{2,1,0:T(8,128)S(1)} all-to-all(f32[16,32,256]{2,1,0:T(8,128)S(1)} %solve.1), channel_id=1, replica_groups=mesh['groups'=2,'tm'=16] {'tm'}, dimensions={0} | all-to-all | bytes 1048576 | tf_op jit(solution)/shard_map/all_to_all | solution.py:276
  55.4 1.0 %copy.10 = f32[2,256,256]{2,1,0:T(8,128)} copy(f32[2,256,256]{1,2,0:T(8,128)S(1)} %bitcast.12) | data formatting | bytes 1048576 | tf_op jit(solution)/shard_map/reshape | solution.py:278
  (4 shorter events, 0.1 us)
Async XLA Ops:
  1.2 0.7 %copy-start.2 = (f32[2]{0:T(128)S(1)}, f32[2]{0:T(128)}, u32[]{:S(2)}) copy-start(f32[2]{0:T(128)} %param.5) | copy-start | bytes 28
  1.3 0.7 %copy-start.1 = (f32[2,256]{1,0:T(2,128)S(1)}, f32[2,256]{1,0:T(2,128)}, u32[]{:S(2)}) copy-start(f32[2,256]{1,0:T(2,128)} %param.6) | copy-start | bytes 6148
  2.1 25.6 %copy-start = (f32[256,256]{1,0:T(8,128)S(1)}, f32[256,256]{1,0:T(8,128)}, u32[]{:S(2)}) copy-start(f32[256,256]{1,0:T(8,128)} %spatial.1) | copy-start | bytes 786436

commit v2 on v1

--- a/solution.py
+++ b/solution.py
@@ -96,12 +96,32 @@
     inverse[...] = 0.5 * (result + result.T)
 
 
+def invert_kernel(spatial, s_high, s_low, g_high, g_low, inverse):
+    s_high[...], s_low[...] = split(spatial[...])
+    invert(spatial[...], inverse)
+    g_high[...], g_low[...] = split(inverse[...])
+
+
+def halves_with_inverse(spatial):
+    size = spatial.shape[0]
+    return pl.pallas_call(
+        invert_kernel,
+        out_shape=[jax.ShapeDtypeStruct((size, size), BF16)] * 4,
+        in_specs=[pl.BlockSpec(memory_space=pltpu.VMEM)],
+        out_specs=[pl.BlockSpec(memory_space=pltpu.VMEM)] * 4,
+        scratch_shapes=[pltpu.VMEM((size, size), F32)],
+        cost_estimate=pl.CostEstimate(flops=48 * size**3, bytes_accessed=16 * size**2, transcendentals=0),
+        compiler_params=pltpu.CompilerParams(vmem_limit_bytes=16 * 2**20),
+        name="invert",
+    )(spatial)
+
+
 def solve_kernel(
     segments, per_segment, columns,
-    received, spatial, out,
-    x, r, p, h, z, q, w, e, d, inverse, s_high, s_low, g_high, g_low,
+    received, s_high, s_low, g_high, g_low, out,
+    x, r, p, h, z, q, w, e, d,
 ):
-    size = spatial.shape[0]
+    size = s_high.shape[0]
     steps = segments * per_segment
     block = per_segment * columns
 
@@ -120,10 +140,6 @@
         if isinstance(t, int):
             return received[i, pl.ds(j * columns, columns), :]
         return received[i, pl.ds(pl.multiple_of(j * columns, SUBLANES), columns), :]
-
-    invert(spatial[...], inverse)
-    s_high[...], s_low[...] = split(spatial[...])
-    g_high[...], g_low[...] = split(inverse[...])
 
     def factor(t, last):
         i, j = source(t)
@@ -232,22 +248,21 @@
     loop(steps, store, 0)
 
 
-def solve(received, spatial, segments, per_segment, columns):
-    size = spatial.shape[0]
+def solve(received, matrices, segments, per_segment, columns):
+    size = received.shape[2]
     steps = segments * per_segment
     rows = steps * columns
     state = pltpu.VMEM((rows, size), F32)
     per_step = pltpu.VMEM((steps, 1, size), F32)
-    matrix = pltpu.VMEM((size, size), BF16)
     return pl.pallas_call(
         functools.partial(solve_kernel, segments, per_segment, columns),
         out_shape=jax.ShapeDtypeStruct((segments, per_segment * columns, size), F32),
-        in_specs=[pl.BlockSpec(memory_space=pltpu.VMEM)] * 2,
+        in_specs=[pl.BlockSpec(memory_space=pltpu.VMEM)] * 5,
         out_specs=pl.BlockSpec(memory_space=pltpu.VMEM),
-        scratch_shapes=[state] * 6 + [per_step] * 3 + [pltpu.VMEM((size, size), F32)] + [matrix] * 4,
+        scratch_shapes=[state] * 6 + [per_step] * 3,
         compiler_params=pltpu.CompilerParams(vmem_limit_bytes=40 * 2**20),
         name="solve",
-    )(received, spatial)
+    )(received, *matrices)
 
 
 def body(spatial, persistence, obs_weight, right_side):
@@ -269,7 +284,7 @@
         block = jnp.pad(block, ((0, 0), (0, 0), (0, padded - columns), (0, 0)))
         block = block.reshape(devices, per_segment * padded, size)
         received = jnp.concatenate([block, received[:, per_segment * columns :]], axis=1)
-    solved = solve(received, spatial, devices, per_segment, padded)
+    solved = solve(received, halves_with_inverse(spatial), devices, per_segment, padded)
     if padded != columns:
         solved = solved.reshape(devices, per_segment, padded, size)[:, :, :columns]
         solved = solved.reshape(devices, per_segment * columns, size)

time: 57.5 us -> 55.8 us (0.970); the launches traced: 56.4 us -> 56 us
  blocking collectives: 43.1 us -> 19 us
  waiting for transfers between devices: 0 us -> 13.6 us
  starting transfers between devices: 0 us -> 7.52 us
  Pallas kernels: 10.1 us -> 11.8 us
  other arithmetic: 0.12 us -> 0.96 us
    all_to_all x1 -> x0, blocking collectives: 25.6 us -> none  [body(): lax.all_to_all(jnp.concatenate([parts, shared], axis=1), 'tm', 0, 0, tile...]
    all_to_all x0 -> x1, waiting for transfers between devices: none -> 13.6 us  [body(): lax.all_to_all(jnp.concatenate([parts, shared], axis=1), 'tm', 0, 0, tile...]
    all_to_all x0 -> x1, starting transfers between devices: none -> 7.52 us  [body(): lax.all_to_all(jnp.concatenate([parts, shared], axis=1), 'tm', 0, 0, tile...]
    pallas_call x0 -> x1, Pallas kernels: none -> 2.94 us  [halves_with_inverse(): pl.pallas_call(invert_kernel, out_shape=[jax.ShapeDtypeStruct((size, size...]
    all_to_all x1, blocking collectives: 17.5 us -> 19 us  [body(): returned = lax.all_to_all(solved, 'tm', 0, 0, tiled=True)]
    pallas_call x1, Pallas kernels: 10.1 us -> 8.83 us  [solve(): pl.pallas_call(functools.partial(solve_kernel, segments, per_segment, col...]
    concatenate x1, other arithmetic: 0.05 us -> 0.89 us  [body(): jnp.concatenate([parts, shared], axis=1)]
  transfers between devices with their start and end apart: 0 -> 1, of which waited for: 0 -> 1; matrix products, arithmetic and copies ran while one was open for 0% -> 0% of each run, Pallas kernels for 0% -> 5%
where the time goes in v2:
time: 55.8 us; the launch traced here: 56 us
  blocking collectives  19 us (34%)
  waiting for transfers between devices  13.6 us (24%)
  Pallas kernels  11.8 us (21%)
  starting transfers between devices  7.52 us (13%)
  local copies, waits for them, and re-layouts  3 us (5%)
  other arithmetic  0.96 us (2%)
    all_to_all x1, blocking collectives, body(): returned = lax.all_to_all(solved, 'tm', 0, 0, tiled=True)  19 us
    all_to_all x1, waiting for transfers between devices, body(): lax.all_to_all(jnp.concatenate([parts, shared], axis=1), 'tm', 0, 0, tile...  13.6 us
    pallas_call x1, Pallas kernels, solve(): pl.pallas_call(functools.partial(solve_kernel, segments, per_segment, col...  8.83 us
    all_to_all x1, starting transfers between devices, body(): lax.all_to_all(jnp.concatenate([parts, shared], axis=1), 'tm', 0, 0, tile...  7.52 us
    pallas_call x1, Pallas kernels, halves_with_inverse(): pl.pallas_call(invert_kernel, out_shape=[jax.ShapeDtypeStruct((size, size...  2.94 us
    unnamed x7, local copies, waits for them, and re-layouts  1.84 us
  transfers between devices with their start and end apart: 1, of which 1 were waited for; matrix products, arithmetic and copies ran while one was open for 0% of the time, Pallas kernels for 5%

profile of v2, /device:TPU:0, one launch (start us, length us, event | category | flops | bytes accessed | tf_op | source)
XLA Modules:
  0.0 56.0 jit_solution(1520249955889481789)
XLA Ops:
  0.0 1.2 %copy.7 = f32[2,256,256]{1,2,0:T(8,128)S(1)} copy(f32[2,256,256]{2,1,0:T(8,128)} %param.7) | data formatting | bytes 1048576 | tf_op args[3]
  1.2 0.0 copy-start.2
  1.3 0.0 copy-start.1
  1.3 0.6 %copy-done.2 = f32[2]{0:T(128)S(1)} copy-done((f32[2]{0:T(128)S(1)}, f32[2]{0:T(128)}, u32[]{:S(2)}) %copy-start.2) | copy-done | bytes 32
  1.9 0.1 pad.8.clone
  2.0 0.0 copy-done.1
  2.0 0.1 pad_maximum_fusion.1
  2.1 0.9 %pad_maximum_fusion = f32[16,40,256]{2,1,0:T(8,128)} fusion(f32[16,8,256]{2,1,0:T(8,128)S(1)} %broadcast_in_dim.5, f32[16,32,256]{2,1,0:T(8,128)S(1)} %bitcast.10), kind=kLoop, calls=%fused_computation | loop fusion | flops 163840 | bytes 1310720 | tf_op jit(solution)/shard_map/concatenate | solution.py:281
  3.0 0.0 copy-start
  3.0 7.5 %all-to-all-start = ((f32[16,40,256]{2,1,0:T(8,128)}), f32[16,40,256]{2,1,0:T(8,128)S(1)}, u32[]{:S(2)}, u32[]{:S(2)}) async-start(f32[16,40,256]{2,1,0:T(8,128)} %pad_maximum_fusion), calls=%async_computation | async-start | bytes 1310720 | tf_op jit(solution)/shard_map/all_to_all | solution.py:281
  10.5 0.0 copy-done
  10.5 2.9 %invert.1 = (bf16[256,256]{1,0:T(8,128)(2,1)S(1)}, bf16[256,256]{1,0:T(8,128)(2,1)S(1)}, bf16[256,256]{1,0:T(8,128)(2,1)S(1)}, bf16[256,256]{1,0:T(8,128)(2,1)S(1)}) custom-call(f32[256,256]{1,0:T(8,128)S(1)} %copy-done), custom_call_target="tpu_custom_call" | custom-call | flops 805306368 | bytes 1048576 | tf_op jit(solution)/shard_map/invert/pallas_call | solution.py:107
  13.4 13.6 %all-to-all-done.received = f32[16,40,256]{2,1,0:T(8,128)S(1)} async-done(((f32[16,40,256]{2,1,0:T(8,128)}), f32[16,40,256]{2,1,0:T(8,128)S(1)}, u32[]{:S(2)}, u32[]{:S(2)}) %all-to-all-start) | async-done | bytes 655392 | tf_op jit(solution)/shard_map/all_to_all | solution.py:281
  27.1 8.8 %solve.1 = f32[16,32,256]{2,1,0:T(8,128)S(1)} custom-call(f32[16,40,256]{2,1,0:T(8,128)S(1)} %all-to-all-done.received, bf16[256,256]{1,0:T(8,128)(2,1)S(1)} %get-tuple-element.9.s_high, bf16[256,256]{1,0:T(8,128)(2,1)S(1)} %get-tuple-element.10.s_low, bf16[256,256]{1,0:T(8,128)(2,1)S(1)} %get-tuple-element.11.g_high, ...), custom_call_target="tpu_custom_call" | custom-call | tf_op jit(solution)/shard_map/solve/pallas_call | solution.py:257
  35.9 19.0 %all_to_all.10 = f32[16,32,256]{2,1,0:T(8,128)S(1)} all-to-all(f32[16,32,256]{2,1,0:T(8,128)S(1)} %solve.1), channel_id=1, replica_groups=mesh['groups'=2,'tm'=16] {'tm'}, dimensions={0} | all-to-all | bytes 1048576 | tf_op jit(solution)/shard_map/all_to_all | solution.py:291
  55.0 1.0 %copy.10 = f32[2,256,256]{2,1,0:T(8,128)} copy(f32[2,256,256]{1,2,0:T(8,128)S(1)} %bitcast.12) | data formatting | bytes 1048576 | tf_op jit(solution)/shard_map/reshape | solution.py:293
  (4 shorter events, 0.1 us)
Async XLA Ops:
  1.2 0.7 %copy-start.2 = (f32[2]{0:T(128)S(1)}, f32[2]{0:T(128)}, u32[]{:S(2)}) copy-start(f32[2]{0:T(128)} %param.5) | copy-start | bytes 28
  1.3 0.7 %copy-start.1 = (f32[2,256]{1,0:T(2,128)S(1)}, f32[2,256]{1,0:T(2,128)}, u32[]{:S(2)}) copy-start(f32[2,256]{1,0:T(2,128)} %param.6) | copy-start | bytes 6148
  3.0 7.5 %copy-start = (f32[256,256]{1,0:T(8,128)S(1)}, f32[256,256]{1,0:T(8,128)}, u32[]{:S(2)}) copy-start(f32[256,256]{1,0:T(8,128)} %spatial.1) | copy-start | bytes 786436
  3.0 24.1 %all-to-all-start = ((f32[16,40,256]{2,1,0:T(8,128)}), f32[16,40,256]{2,1,0:T(8,128)S(1)}, u32[]{:S(2)}, u32[]{:S(2)}) async-start(f32[16,40,256]{2,1,0:T(8,128)} %pad_maximum_fusion), calls=%async_computation | async-start | bytes 1310720 | tf_op jit(solution)/shard_map/all_to_all | solution.py:281

commit v3 on v1

v3 whole, which is shorter than its diff:
```python
import functools

import jax
import jax.numpy as jnp
from jax import lax
from jax.experimental import pallas as pl
from jax.experimental.pallas import tpu as pltpu
from jax.sharding import PartitionSpec as P

F32 = jnp.float32
BF16 = jnp.bfloat16
SUBLANES = 8
LANES = 128
TOLERANCE = 1e-5
STEP_LIMIT = 2000
COARSE_LIMIT = 14
FINE_LIMIT = 80
INVERSE_TOLERANCE = 1e-5
CORRECTION_TOLERANCE = 1e-6
REFINEMENT_LIMIT = 8


def split(value):
    high = value.astype(BF16)
    return high, (value - high.astype(F32)).astype(BF16)


def dot(left, right):
    return jnp.dot(left, right, preferred_element_type=F32)


def split_dot(left, right_high, right_low):
    high, low = split(left)
    return dot(high, right_high) + dot(low, right_high) + dot(high, right_low)


def exact_dot(left, right):
    return jnp.dot(left, right, preferred_element_type=F32, precision=lax.Precision.HIGHEST)


def loop(count, body, start):
    if count <= 32:
        carry = start
        for i in range(count):
            carry = body(i, carry)
        return carry
    return lax.fori_loop(0, count, body, start)


def eye(size):
    rows = lax.broadcasted_iota(jnp.int32, (size, size), 0)
    columns = lax.broadcasted_iota(jnp.int32, (size, size), 1)
    return jnp.where(rows == columns, 1.0, 0.0).astype(F32)


def row_sum_norm(value):
    return jnp.max(jnp.sum(jnp.abs(value), axis=0, keepdims=True))


def invert(spatial, inverse):
    size = spatial.shape[0]
    identity = eye(size)
    high = spatial.astype(BF16)
    square = dot(high, high)
    bound = jnp.sqrt(row_sum_norm(square)) * 1.02
    scale = 1.9 / bound
    start = scale * (2.0 * identity - scale * spatial)
    inverse[...] = start

    def coarse_step(state):
        count, unused = state
        guess = inverse[...]
        residual = identity - dot(high, guess.astype(BF16))
        inverse[...] = guess + dot(guess.astype(BF16), residual.astype(BF16))
        return count + 1, row_sum_norm(residual)

    def coarse_goes_on(state):
        count, error = state
        return jnp.logical_and(count < COARSE_LIMIT, error > 0.3)

    unused, error = lax.while_loop(coarse_goes_on, coarse_step, (0, F32(1e30)))

    @pl.when(jnp.logical_not(error <= 0.3))
    def restart():
        inverse[...] = start

    def fine_step(state):
        count, unused = state
        guess = inverse[...]
        residual = identity - exact_dot(spatial, guess)
        inverse[...] = guess + exact_dot(guess, residual)
        return count + 1, row_sum_norm(residual)

    def fine_goes_on(state):
        count, error = state
        return jnp.logical_and(count < FINE_LIMIT, error > 1e-3)

    lax.while_loop(fine_goes_on, fine_step, (0, F32(1e30)))
    result = inverse[...]
    result = 0.5 * (result + result.T)
    inverse[...] = result
    residual = identity - exact_dot(spatial, result)
    return jnp.sum(residual * residual) / size


def invert_kernel(spatial, inverse, high, low, error):
    error[0, 0] = invert(spatial[...], inverse)
    high[...], low[...] = split(inverse[...])


def invert_spatial(spatial):
    size = spatial.shape[0]
    half = jax.ShapeDtypeStruct((size, size), BF16)
    full = jax.ShapeDtypeStruct((size, size), F32)
    vmem, smem = pl.BlockSpec(memory_space=pltpu.VMEM), pl.BlockSpec(memory_space=pltpu.SMEM)
    return pl.pallas_call(
        invert_kernel,
        out_shape=[full, half, half, jax.ShapeDtypeStruct((1, 1), F32)],
        in_specs=[vmem],
        out_specs=[vmem, vmem, vmem, smem],
        cost_estimate=pl.CostEstimate(flops=80 * size**3, bytes_accessed=16 * size**2, transcendentals=0),
        compiler_params=pltpu.CompilerParams(vmem_limit_bytes=16 * 2**20),
        name="invert",
    )(spatial)


def pack_kernel(rates, right_side, weights, out):
    steps, size, column_count = right_side.shape
    devices = out.shape[0]
    columns = column_count // devices
    halves = size // LANES
    tail = steps * halves * columns
    for e in range(steps):
        turned = right_side[e].T
        for i in range(devices):
            for k in range(halves):
                out[i, pl.ds((e * halves + k) * columns, columns), :] = turned[
                    i * columns : (i + 1) * columns, k * LANES : (k + 1) * LANES
                ]
    row = lax.broadcasted_iota(jnp.int32, (out.shape[1] - tail, LANES), 0)
    last = jnp.zeros(row.shape, F32)
    for e in range(steps):
        for k in range(halves):
            weight = weights[pl.ds(e, 1), pl.ds(k * LANES, LANES)]
            last = jnp.where(row == e * halves + k, weight, last)
        last = jnp.where(row == steps * halves + e, rates[e], last)
    for i in range(devices):
        out[i, pl.ds(tail, row.shape[0]), :] = last


def pack(persistence, right_side, weights, devices):
    steps, size, column_count = right_side.shape
    halves = size // LANES
    rows = steps * halves * (column_count // devices)
    total = rows + steps * halves + steps
    total += -total % SUBLANES
    vmem, smem = pl.BlockSpec(memory_space=pltpu.VMEM), pl.BlockSpec(memory_space=pltpu.SMEM)
    return pl.pallas_call(
        pack_kernel,
        out_shape=jax.ShapeDtypeStruct((devices, total, LANES), F32),
        in_specs=[smem, vmem, vmem],
        out_specs=vmem,
        compiler_params=pltpu.CompilerParams(vmem_limit_bytes=16 * 2**20),
        name="pack",
    )(persistence, right_side, weights)


def solve_kernel(
    segments, per_segment, columns,
    received, error, spatial, g, g_high, g_low, out,
    x, r, p, z, w, e, d, rates,
):
    size = g.shape[0]
    steps = segments * per_segment
    halves = size // LANES
    tail = per_segment * halves * columns

    def rows(start):
        if isinstance(start, int):
            return pl.ds(start, columns)
        return pl.ds(pl.multiple_of(start, SUBLANES), columns)

    def at(t):
        return rows(t * columns)

    def source(t):
        if isinstance(t, int):
            return t // per_segment, t % per_segment
        return lax.div(t, per_segment), lax.rem(t, per_segment)

    def lanes(pieces):
        return jnp.concatenate(pieces, axis=1)

    def right_side(t):
        i, j = source(t)
        return lanes([received[i, rows((j * halves + k) * columns), :] for k in range(halves)])

    def over_lanes(value):
        return jnp.sum(value, axis=1, keepdims=True)

    def zero():
        return jnp.zeros((columns, size), F32)

    def ratio(top, bottom):
        return jnp.where(bottom > 0.0, top / jnp.where(bottom > 0.0, bottom, 1.0), 0.0)

    def factor(t, last):
        i, j = source(t)
        w[t] = lanes([received[i, pl.ds(tail + j * halves + k, 1), :] for k in range(halves)])
        rate = received[i, pl.ds(tail + per_segment * halves + j, 1), :]
        link = rate * last
        inverse_pivot = 1.0 / (1.0 + rate * rate - rate * link)
        rates[t] = lanes([rate] * halves)
        e[t] = lanes([link] * halves)
        d[t] = lanes([inverse_pivot] * halves)
        return inverse_pivot

    loop(steps, factor, jnp.zeros((1, LANES), F32))

    biggest = loop(steps, lambda t, acc: jnp.maximum(acc, jnp.abs(right_side(t))), zero())
    biggest = jnp.max(biggest, axis=1, keepdims=True)
    biggest = jnp.where(biggest > 0.0, biggest, 1.0)
    shrink = 1.0 / biggest

    def load(t, carry):
        r[at(t), :] = right_side(t) * shrink
        return carry

    loop(steps, load, 0)

    def down(t, last):
        value = z[at(t), :] + e[t] * last
        z[at(t), :] = value
        return value

    def start(first):
        z[...] = exact_dot(r[...], g[...])
        loop(steps, down, zero())

        def up(k, carry):
            above, acc = carry
            t = steps - 1 - k
            value = z[at(t), :] * d[t] + above
            x[at(t), :] = value if first else x[at(t), :] + value
            r[at(t), :] = value
            p[at(t), :] = value
            return e[t] * value, acc + w[t] * value * value

        unused, acc = loop(steps, up, (zero(), zero()))
        return over_lanes(acc)

    def weigh(t, carry):
        z[at(t), :] = w[t] * p[at(t), :]
        return carry

    def step(state):
        count, square, limit, unused = state
        loop(steps, weigh, 0)
        z[...] = split_dot(z[...], g_high[...], g_low[...])
        loop(steps, down, zero())

        def up(k, carry):
            above, own, cross = carry
            t = steps - 1 - k
            value = z[at(t), :] * d[t] + above
            z[at(t), :] = value
            direction = p[at(t), :]
            weighted = w[t] * direction
            return e[t] * value, own + weighted * direction, cross + weighted * value

        unused, own, cross = loop(steps, up, (zero(), zero(), zero()))
        own, cross = over_lanes(own), over_lanes(cross)
        alpha = ratio(square, own + cross)

        def advance(t, acc):
            change = z[at(t), :]
            x[at(t), :] -= alpha * change
            value = r[at(t), :] - alpha * (p[at(t), :] + change)
            r[at(t), :] = value
            return acc + w[t] * value * value

        new_square = over_lanes(loop(steps, advance, zero()))
        beta = ratio(new_square, square)

        def turn(t, carry):
            p[at(t), :] = r[at(t), :] + beta * p[at(t), :]
            return carry

        loop(steps, turn, 0)
        share = ratio(cross, own + cross)
        return count + 1, new_square, limit, jnp.max(share * share * new_square - limit)

    def goes_on(state):
        count, unused, unused_limit, excess = state
        return jnp.logical_and(count < STEP_LIMIT, excess > 0.0)

    def iterate(square):
        lax.while_loop(goes_on, step, (0, square, square * TOLERANCE**2, jnp.max(square)))

    whole_square = start(True)
    iterate(whole_square)

    def refine(state):
        count, unused = state

        def combine(t, last):
            here = x[at(t), :]
            after = jnp.minimum(t + 1, steps - 1)
            link = jnp.where(t + 1 < steps, 1.0, 0.0) * rates[after]
            value = (1.0 + rates[t] * rates[t]) * here - rates[t] * last - link * x[at(after), :]
            z[at(t), :] = value
            return here

        lax.fori_loop(0, steps, combine, zero())
        z[...] = exact_dot(z[...], spatial[...])

        def subtract(t, carry):
            i, j = source(t)
            r[at(t), :] = right_side(t) * shrink - z[at(t), :] - w[t] * x[at(t), :]
            return carry

        lax.fori_loop(0, steps, subtract, 0)
        square = start(False)
        iterate(square)
        return count + 1, jnp.max(square - whole_square * CORRECTION_TOLERANCE**2)

    def refines(state):
        count, excess = state
        return jnp.logical_and(count < REFINEMENT_LIMIT, excess > 0.0)

    lax.while_loop(refines, refine, (0, error[0, 0] - INVERSE_TOLERANCE**2))

    def store(t, carry):
        i, j = source(t)
        out[i, rows(j * columns), :] = x[at(t), :] * biggest
        return carry

    loop(steps, store, 0)


def solve(received, spatial, inverse, segments, per_segment, columns):
    size = spatial.shape[0]
    steps = segments * per_segment
    state = pltpu.VMEM((steps * columns, size), F32)
    per_step = pltpu.VMEM((steps, 1, size), F32)
    full, high, low, error = inverse
    vmem, smem = pl.BlockSpec(memory_space=pltpu.VMEM), pl.BlockSpec(memory_space=pltpu.SMEM)
    return pl.pallas_call(
        functools.partial(solve_kernel, segments, per_segment, columns),
        out_shape=jax.ShapeDtypeStruct((segments, per_segment * columns, size), F32),
        in_specs=[vmem, smem, vmem, vmem, vmem, vmem],
        out_specs=vmem,
        scratch_shapes=[state] * 4 + [per_step] * 4,
        compiler_params=pltpu.CompilerParams(vmem_limit_bytes=40 * 2**20),
        name="solve",
    )(received, error, spatial, full, high, low)


def pad_columns(received, per_segment, halves, columns, padded):
    devices, total, width = received.shape
    rows = per_segment * halves * columns
    block = received[:, :rows].reshape(devices, per_segment * halves, columns, width)
    block = jnp.pad(block, ((0, 0), (0, 0), (0, padded - columns), (0, 0)))
    return jnp.concatenate([block.reshape(devices, -1, width), received[:, rows:]], axis=1)


def body(spatial, persistence, obs_weight, right_side):
    devices = lax.axis_size("tm")
    per_segment, size, column_count = right_side.shape
    columns = column_count // devices
    padded = -(-columns // SUBLANES) * SUBLANES
    inverse = invert_spatial(spatial)
    packed = pack(persistence, right_side, obs_weight, devices)
    received = lax.all_to_all(packed, "tm", 0, 0, tiled=True)
    if padded != columns:
        received = pad_columns(received, per_segment, size // LANES, columns, padded)
    solved = solve(received, spatial, inverse, devices, per_segment, padded)
    if padded != columns:
        solved = solved.reshape(devices, per_segment, padded, size)[:, :, :columns]
        solved = solved.reshape(devices, per_segment * columns, size)
    returned = lax.all_to_all(solved, "tm", 0, 0, tiled=True)
    returned = returned.reshape(devices, per_segment, columns, size)
    return jnp.transpose(returned, (1, 3, 0, 2)).reshape(per_segment, size, column_count)


def solution(mesh):
    placed = (P(), P(("groups", "tm")), P(("groups", "tm"), None), P(("groups", "tm"), None, None))
    return jax.shard_map(
        body, mesh=mesh, in_specs=placed, out_specs=P(("groups", "tm"), None, None), check_vma=False
    )
```

time: 57.5 us -> 51.3 us (0.89); the launches traced: 56.4 us -> 51 us
  blocking collectives: 43.1 us -> 18.7 us
  waiting for transfers between devices: 0 us -> 10.5 us
  starting transfers between devices: 0 us -> 7.52 us
  Pallas kernels: 10.1 us -> 10.8 us
    all_to_all x1 -> x0, blocking collectives: 25.6 us -> none  [body(): lax.all_to_all(jnp.concatenate([parts, shared], axis=1), 'tm', 0, 0, tile...]
    all_to_all x0 -> x1, waiting for transfers between devices: none -> 10.5 us  [body(): received = lax.all_to_all(packed, 'tm', 0, 0, tiled=True)]
    all_to_all x0 -> x1, starting transfers between devices: none -> 7.52 us  [body(): received = lax.all_to_all(packed, 'tm', 0, 0, tiled=True)]
    pallas_call x0 -> x2, Pallas kernels: none -> 6.62 us  [the longest x1 5.06 us: invert_spatial(): pl.pallas_call(invert_kernel, out_shape=[full, half, half, jax.ShapeDtype...]
    pallas_call x1, Pallas kernels: 10.1 us -> 4.2 us  [solve(): pl.pallas_call(functools.partial(solve_kernel, segments, per_segment, col...]
    all_to_all x1, blocking collectives: 17.5 us -> 18.7 us  [body(): returned = lax.all_to_all(solved, 'tm', 0, 0, tiled=True)]
    unnamed x7 -> x8, local copies, waits for them, and re-layouts: 1.84 us -> 2.38 us
  transfers between devices with their start and end apart: 0 -> 1, of which waited for: 0 -> 1; matrix products, arithmetic and copies ran while one was open for 0% -> 0% of each run, Pallas kernels for 0% -> 10%
where the time goes in v3:
time: 51.3 us; the launch traced here: 51 us
  blocking collectives  18.7 us (36%)
  Pallas kernels  10.8 us (21%)
  waiting for transfers between devices  10.5 us (20%)
  starting transfers between devices  7.52 us (15%)
  local copies, waits for them, and re-layouts  3.41 us (7%)
    all_to_all x1, blocking collectives, body(): returned = lax.all_to_all(solved, 'tm', 0, 0, tiled=True)  18.7 us
    all_to_all x1, waiting for transfers between devices, body(): received = lax.all_to_all(packed, 'tm', 0, 0, tiled=True)  10.5 us
    all_to_all x1, starting transfers between devices, body(): received = lax.all_to_all(packed, 'tm', 0, 0, tiled=True)  7.52 us
    pallas_call x1, Pallas kernels, invert_spatial(): pl.pallas_call(invert_kernel, out_shape=[full, half, half, jax.ShapeDtype...  5.06 us
    pallas_call x1, Pallas kernels, solve(): pl.pallas_call(functools.partial(solve_kernel, segments, per_segment, col...  4.2 us
    unnamed x8, local copies, waits for them, and re-layouts  2.38 us
    pallas_call x1, Pallas kernels, pack(): pl.pallas_call(pack_kernel, out_shape=jax.ShapeDtypeStruct((devices, tota...  1.56 us
  transfers between devices with their start and end apart: 1, of which 1 were waited for; matrix products, arithmetic and copies ran while one was open for 0% of the time, Pallas kernels for 10%

profile of v3, /device:TPU:0, one launch (start us, length us, event | category | flops | bytes accessed | tf_op | source)
XLA Modules:
  0.0 51.0 jit_solution(5536699859716711680)
XLA Ops:
  0.0 0.0 copy-start
  0.0 1.0 %copy-done = f32[2,256,256]{2,1,0:T(8,128)S(1)} copy-done((f32[2,256,256]{2,1,0:T(8,128)S(1)}, f32[2,256,256]{2,1,0:T(8,128)}, u32[]{:S(2)}) %copy-start) | copy-done | bytes 524312
  1.0 0.0 copy-start.2
  1.0 0.7 %copy-done.2 = f32[2,256]{1,0:T(2,128)S(1)} copy-done((f32[2,256]{1,0:T(2,128)S(1)}, f32[2,256]{1,0:T(2,128)}, u32[]{:S(2)}) %copy-start.2) | copy-done | bytes 2072
  1.7 0.0 copy-start.3
  1.7 0.7 %copy-done.3 = f32[2]{0:T(128)S(1)} copy-done((f32[2]{0:T(128)S(1)}, f32[2]{0:T(128)}, u32[]{:S(2)}) %copy-start.3) | copy-done | bytes 32
  2.4 1.6 %pack.1 = f32[16,72,128]{2,1,0:T(8,128)} custom-call(f32[2]{0:T(128)S(1)} %copy-done.3, f32[2,256,256]{2,1,0:T(8,128)S(1)} %copy-done, f32[2,256]{1,0:T(2,128)S(1)} %copy-done.2), custom_call_target="tpu_custom_call" | custom-call | tf_op jit(solution)/shard_map/pack/pallas_call | solution.py:158
  3.9 0.0 copy-start.1
  3.9 7.5 %all-to-all-start = ((f32[16,72,128]{2,1,0:T(8,128)}), f32[16,72,128]{2,1,0:T(8,128)S(1)}, u32[]{:S(2)}, u32[]{:S(2)}) async-start(f32[16,72,128]{2,1,0:T(8,128)} %pack.1), calls=%async_computation | async-start | bytes 1179648 | tf_op jit(solution)/shard_map/all_to_all | solution.py:374
  11.5 0.0 copy-done.1
  11.5 5.1 %invert.1 = (f32[256,256]{1,0:T(8,128)S(1)}, bf16[256,256]{1,0:T(8,128)(2,1)S(1)}, bf16[256,256]{1,0:T(8,128)(2,1)S(1)}, f32[1,1]{1,0:T(1,128)}) custom-call(f32[256,256]{1,0:T(8,128)S(1)} %copy-done.1), custom_call_target="tpu_custom_call" | custom-call | flops 1342177280 | bytes 1048576 | tf_op jit(solution)/shard_map/invert/pallas_call | solution.py:116
  16.5 10.5 %all-to-all-done.received = f32[16,72,128]{2,1,0:T(8,128)S(1)} async-done(((f32[16,72,128]{2,1,0:T(8,128)}), f32[16,72,128]{2,1,0:T(8,128)S(1)}, u32[]{:S(2)}, u32[]{:S(2)}) %all-to-all-start) | async-done | bytes 589856 | tf_op jit(solution)/shard_map/all_to_all | solution.py:374
  27.0 4.2 %solve.1 = f32[16,32,256]{2,1,0:T(8,128)S(1)} custom-call(f32[16,72,128]{2,1,0:T(8,128)S(1)} %all-to-all-done.received, f32[1,1]{1,0:T(1,128)} %get-tuple-element.9.error, f32[256,256]{1,0:T(8,128)S(1)} %copy-done.1, f32[256,256]{1,0:T(8,128)S(1)} %get-tuple-element.10.g, bf16[256,256]{1,0:T(8,128)(2,1)S(1)} %get-tuple-element.11.g_high, ...), custom_call_target="tpu_custom_call" | custom-call | tf_op jit(solution)/shard_map/solve/pallas_call | solution.py:348
  31.2 18.7 %all_to_all.10 = f32[16,32,256]{2,1,0:T(8,128)S(1)} all-to-all(f32[16,32,256]{2,1,0:T(8,128)S(1)} %solve.1), channel_id=1, replica_groups=mesh['groups'=2,'tm'=16] {'tm'}, dimensions={0} | all-to-all | bytes 1048576 | tf_op jit(solution)/shard_map/all_to_all | solution.py:381
  50.0 1.0 %copy.7 = f32[2,256,256]{2,1,0:T(8,128)} copy(f32[2,256,256]{1,2,0:T(8,128)S(1)} %bitcast.5) | data formatting | bytes 1048576 | tf_op jit(solution)/shard_map/reshape | solution.py:383
  (1 shorter events, 0.0 us)
Async XLA Ops:
  0.0 1.0 %copy-start = (f32[2,256,256]{2,1,0:T(8,128)S(1)}, f32[2,256,256]{2,1,0:T(8,128)}, u32[]{:S(2)}) copy-start(f32[2,256,256]{2,1,0:T(8,128)} %right_side.1) | copy-start | bytes 1572868
  1.0 0.7 %copy-start.2 = (f32[2,256]{1,0:T(2,128)S(1)}, f32[2,256]{1,0:T(2,128)}, u32[]{:S(2)}) copy-start(f32[2,256]{1,0:T(2,128)} %weights.1) | copy-start | bytes 6148
  1.7 0.7 %copy-start.3 = (f32[2]{0:T(128)S(1)}, f32[2]{0:T(128)}, u32[]{:S(2)}) copy-start(f32[2]{0:T(128)} %rates.1) | copy-start | bytes 28
  3.9 7.5 %copy-start.1 = (f32[256,256]{1,0:T(8,128)S(1)}, f32[256,256]{1,0:T(8,128)}, u32[]{:S(2)}) copy-start(f32[256,256]{1,0:T(8,128)} %spatial.3) | copy-start | bytes 786436
  3.9 23.1 %all-to-all-start = ((f32[16,72,128]{2,1,0:T(8,128)}), f32[16,72,128]{2,1,0:T(8,128)S(1)}, u32[]{:S(2)}, u32[]{:S(2)}) async-start(f32[16,72,128]{2,1,0:T(8,128)} %pack.1), calls=%async_computation | async-start | bytes 1179648 | tf_op jit(solution)/shard_map/all_to_all | solution.py:374

commit v4 on v3

--- a/solution.py
+++ b/solution.py
@@ -11,11 +11,13 @@
 BF16 = jnp.bfloat16
 SUBLANES = 8
 LANES = 128
+CHUNKS = 1
 TOLERANCE = 1e-5
 STEP_LIMIT = 2000
 COARSE_LIMIT = 14
 FINE_LIMIT = 80
 INVERSE_TOLERANCE = 1e-5
+EASY_STEPS = 6
 CORRECTION_TOLERANCE = 1e-6
 REFINEMENT_LIMIT = 8
 
@@ -124,56 +126,89 @@
     )(spatial)
 
 
-def pack_kernel(rates, right_side, weights, out):
+def tail_rows(per_segment, halves):
+    rows = per_segment * halves + per_segment
+    return rows + -rows % SUBLANES
+
+
+def pack_kernel(chunks, rates, right_side, weights, *refs):
+    outs, (turned, source, rate, weight, arrivals, departures) = refs[:chunks], refs[chunks:]
     steps, size, column_count = right_side.shape
-    devices = out.shape[0]
+    devices = outs[0].shape[0]
     columns = column_count // devices
+    part = columns // chunks
     halves = size // LANES
-    tail = steps * halves * columns
-    for e in range(steps):
-        turned = right_side[e].T
-        for i in range(devices):
-            for k in range(halves):
-                out[i, pl.ds((e * halves + k) * columns, columns), :] = turned[
-                    i * columns : (i + 1) * columns, k * LANES : (k + 1) * LANES
-                ]
-    row = lax.broadcasted_iota(jnp.int32, (out.shape[1] - tail, LANES), 0)
+    block = steps * halves * part
+    tail = tail_rows(steps, halves)
+    loads = [pltpu.make_async_copy(right_side.at[e], source.at[e], arrivals.at[e]) for e in range(steps)]
+    loads.append(pltpu.make_async_copy(rates, rate, arrivals.at[steps]))
+    loads.append(pltpu.make_async_copy(weights, weight, arrivals.at[steps + 1]))
+    for copy in loads:
+        copy.start()
+    for copy in loads[steps:]:
+        copy.wait()
+    row = lax.broadcasted_iota(jnp.int32, (tail, LANES), 0)
     last = jnp.zeros(row.shape, F32)
     for e in range(steps):
         for k in range(halves):
-            weight = weights[pl.ds(e, 1), pl.ds(k * LANES, LANES)]
-            last = jnp.where(row == e * halves + k, weight, last)
-        last = jnp.where(row == steps * halves + e, rates[e], last)
+            last = jnp.where(row == e * halves + k, weight[pl.ds(e, 1), pl.ds(k * LANES, LANES)], last)
+        last = jnp.where(row == steps * halves + e, rate[e], last)
     for i in range(devices):
-        out[i, pl.ds(tail, row.shape[0]), :] = last
-
-
-def pack(persistence, right_side, weights, devices):
+        turned[0, i, pl.ds(block, tail), :] = last
+    for e in range(steps):
+        loads[e].wait()
+        value = source[e].T
+        for i in range(devices):
+            for c in range(chunks):
+                for k in range(halves):
+                    first = i * columns + c * part
+                    turned[c, i, pl.ds((e * halves + k) * part, part), :] = value[
+                        first : first + part, k * LANES : (k + 1) * LANES
+                    ]
+    stores = [
+        pltpu.make_async_copy(turned.at[c, :, pl.ds(0, out.shape[1]), :], out, departures.at[c])
+        for c, out in enumerate(outs)
+    ]
+    for copy in stores:
+        copy.start()
+    for copy in stores:
+        copy.wait()
+
+
+def pack(persistence, right_side, weights, devices, chunks):
     steps, size, column_count = right_side.shape
     halves = size // LANES
-    rows = steps * halves * (column_count // devices)
-    total = rows + steps * halves + steps
-    total += -total % SUBLANES
-    vmem, smem = pl.BlockSpec(memory_space=pltpu.VMEM), pl.BlockSpec(memory_space=pltpu.SMEM)
+    rows = steps * halves * (column_count // devices // chunks)
+    total = rows + tail_rows(steps, halves)
+    anywhere = pl.BlockSpec(memory_space=pl.ANY)
+    shapes = [total] + [rows] * (chunks - 1)
     return pl.pallas_call(
-        pack_kernel,
-        out_shape=jax.ShapeDtypeStruct((devices, total, LANES), F32),
-        in_specs=[smem, vmem, vmem],
-        out_specs=vmem,
-        compiler_params=pltpu.CompilerParams(vmem_limit_bytes=16 * 2**20),
+        functools.partial(pack_kernel, chunks),
+        out_shape=[jax.ShapeDtypeStruct((devices, n, LANES), F32) for n in shapes],
+        in_specs=[anywhere] * 3,
+        out_specs=[anywhere] * chunks,
+        scratch_shapes=[
+            pltpu.VMEM((chunks, devices, total, LANES), F32),
+            pltpu.VMEM(right_side.shape, F32),
+            pltpu.SMEM(persistence.shape, F32),
+            pltpu.VMEM(weights.shape, F32),
+            pltpu.SemaphoreType.DMA((steps + 2,)),
+            pltpu.SemaphoreType.DMA((chunks,)),
+        ],
+        compiler_params=pltpu.CompilerParams(vmem_limit_bytes=56 * 2**20),
         name="pack",
     )(persistence, right_side, weights)
 
 
 def solve_kernel(
     segments, per_segment, columns,
-    received, error, spatial, g, g_high, g_low, out,
+    received, shared, error, spatial, g, g_high, g_low, out,
     x, r, p, z, w, e, d, rates,
 ):
     size = g.shape[0]
     steps = segments * per_segment
     halves = size // LANES
-    tail = per_segment * halves * columns
+    tail = shared.shape[1] - tail_rows(per_segment, halves)
 
     def rows(start):
         if isinstance(start, int):
@@ -206,8 +241,8 @@
 
     def factor(t, last):
         i, j = source(t)
-        w[t] = lanes([received[i, pl.ds(tail + j * halves + k, 1), :] for k in range(halves)])
-        rate = received[i, pl.ds(tail + per_segment * halves + j, 1), :]
+        w[t] = lanes([shared[i, pl.ds(tail + j * halves + k, 1), :] for k in range(halves)])
+        rate = shared[i, pl.ds(tail + per_segment * halves + j, 1), :]
         link = rate * last
         inverse_pivot = 1.0 / (1.0 + rate * rate - rate * link)
         rates[t] = lanes([rate] * halves)
@@ -295,10 +330,10 @@
         return jnp.logical_and(count < STEP_LIMIT, excess > 0.0)
 
     def iterate(square):
-        lax.while_loop(goes_on, step, (0, square, square * TOLERANCE**2, jnp.max(square)))
+        return lax.while_loop(goes_on, step, (0, square, square * TOLERANCE**2, jnp.max(square)))[0]
 
     whole_square = start(True)
-    iterate(whole_square)
+    count = iterate(whole_square)
 
     def refine(state):
         count, unused = state
@@ -328,7 +363,8 @@
         count, excess = state
         return jnp.logical_and(count < REFINEMENT_LIMIT, excess > 0.0)
 
-    lax.while_loop(refines, refine, (0, error[0, 0] - INVERSE_TOLERANCE**2))
+    needed = jnp.logical_or(error[0, 0] > INVERSE_TOLERANCE**2, count > EASY_STEPS)
+    lax.while_loop(refines, refine, (0, jnp.where(needed, 1.0, 0.0)))
 
     def store(t, carry):
         i, j = source(t)
@@ -338,7 +374,7 @@
     loop(steps, store, 0)
 
 
-def solve(received, spatial, inverse, segments, per_segment, columns):
+def solve(received, shared, spatial, inverse, segments, per_segment, columns):
     size = spatial.shape[0]
     steps = segments * per_segment
     state = pltpu.VMEM((steps * columns, size), F32)
@@ -348,12 +384,12 @@
     return pl.pallas_call(
         functools.partial(solve_kernel, segments, per_segment, columns),
         out_shape=jax.ShapeDtypeStruct((segments, per_segment * columns, size), F32),
-        in_specs=[vmem, smem, vmem, vmem, vmem, vmem],
+        in_specs=[vmem, vmem, smem, vmem, vmem, vmem, vmem],
         out_specs=vmem,
         scratch_shapes=[state] * 4 + [per_step] * 4,
         compiler_params=pltpu.CompilerParams(vmem_limit_bytes=40 * 2**20),
         name="solve",
-    )(received, error, spatial, full, high, low)
+    )(received, shared, error, spatial, full, high, low)
 
 
 def pad_columns(received, per_segment, halves, columns, padded):
@@ -367,20 +403,25 @@
 def body(spatial, persistence, obs_weight, right_side):
     devices = lax.axis_size("tm")
     per_segment, size, column_count = right_side.shape
-    columns = column_count // devices
+    halves = size // LANES
+    chunks = CHUNKS if column_count // devices % (CHUNKS * SUBLANES) == 0 else 1
+    columns = column_count // devices // chunks
     padded = -(-columns // SUBLANES) * SUBLANES
     inverse = invert_spatial(spatial)
-    packed = pack(persistence, right_side, obs_weight, devices)
-    received = lax.all_to_all(packed, "tm", 0, 0, tiled=True)
-    if padded != columns:
-        received = pad_columns(received, per_segment, size // LANES, columns, padded)
-    solved = solve(received, spatial, inverse, devices, per_segment, padded)
-    if padded != columns:
-        solved = solved.reshape(devices, per_segment, padded, size)[:, :, :columns]
-        solved = solved.reshape(devices, per_segment * columns, size)
-    returned = lax.all_to_all(solved, "tm", 0, 0, tiled=True)
-    returned = returned.reshape(devices, per_segment, columns, size)
-    return jnp.transpose(returned, (1, 3, 0, 2)).reshape(per_segment, size, column_count)
+    packed = pack(persistence, right_side, obs_weight, devices, chunks)
+    received = [lax.all_to_all(chunk, "tm", 0, 0, tiled=True) for chunk in packed]
+    returned = []
+    for chunk in received:
+        if padded != columns:
+            chunk = pad_columns(chunk, per_segment, halves, columns, padded)
+        solved = solve(chunk, received[0], spatial, inverse, devices, per_segment, padded)
+        if padded != columns:
+            solved = solved.reshape(devices, per_segment, padded, size)[:, :, :columns]
+            solved = solved.reshape(devices, per_segment * columns, size)
+        solved = lax.all_to_all(solved, "tm", 0, 0, tiled=True)
+        returned.append(solved.reshape(devices, per_segment, columns, size))
+    returned = jnp.stack(returned, axis=2)
+    return jnp.transpose(returned, (1, 4, 0, 2, 3)).reshape(per_segment, size, column_count)
 
 
 def solution(mesh):

time: 51.3 us -> 49.8 us (0.971)
  local copies, waits for them, and re-layouts: 3.41 us -> 1.04 us
    unnamed x8 -> x2, local copies, waits for them, and re-layouts: 2.38 us -> 0.01 us
    pallas_call x1, Pallas kernels: 1.56 us -> 2.08 us  [pack(): pl.pallas_call(functools.partial(pack_kernel, chunks), out_shape=[jax.Sha...]
    reshape x2 -> x1, local copies, waits for them, and re-layouts: 1.03 us -> 1 us  [body(): jnp.transpose(returned, (1, 4, 0, 2, 3))]
where the time goes in v4:
time: 49.8 us; the launch traced here: 49.1 us
  blocking collectives  18.7 us (38%)
  Pallas kernels  11.3 us (23%)
  waiting for transfers between devices  10.5 us (21%)
  starting transfers between devices  7.53 us (15%)
  local copies, waits for them, and re-layouts  1.04 us (2%)
    all_to_all x1, blocking collectives, body(): solved = lax.all_to_all(solved, 'tm', 0, 0, tiled=True)  18.7 us
    all_to_all x1, waiting for transfers between devices, body(): lax.all_to_all(chunk, 'tm', 0, 0, tiled=True)  10.5 us
    all_to_all x1, starting transfers between devices, body(): lax.all_to_all(chunk, 'tm', 0, 0, tiled=True)  7.53 us
    pallas_call x1, Pallas kernels, invert_spatial(): pl.pallas_call(invert_kernel, out_shape=[full, half, half, jax.ShapeDtype...  5.06 us
    pallas_call x1, Pallas kernels, solve(): pl.pallas_call(functools.partial(solve_kernel, segments, per_segment, col...  4.2 us
    pallas_call x1, Pallas kernels, pack(): pl.pallas_call(functools.partial(pack_kernel, chunks), out_shape=[jax.Sha...  2.08 us
  transfers between devices with their start and end apart: 1, of which 1 were waited for; matrix products, arithmetic and copies ran while one was open for 0% of the time, Pallas kernels for 10%

profile of v4, /device:TPU:0, one launch (start us, length us, event | category | flops | bytes accessed | tf_op | source)
XLA Modules:
  0.0 49.1 jit_solution(11064671552057412846)
XLA Ops:
  0.0 2.1 %pack.1 = f32[16,72,128]{2,1,0:T(8,128)} custom-call(f32[2]{0:T(128)} %rates.1, f32[2,256,256]{2,1,0:T(8,128)} %right_side.1, f32[2,256]{1,0:T(2,128)} %weights.1), custom_call_target="tpu_custom_call" | custom-call | tf_op jit(solution)/shard_map/pack/pallas_call | solution.py:185
  2.1 0.0 copy-start
  2.1 7.5 %all-to-all-start = ((f32[16,72,128]{2,1,0:T(8,128)}), f32[16,72,128]{2,1,0:T(8,128)S(1)}, u32[]{:S(2)}, u32[]{:S(2)}) async-start(f32[16,72,128]{2,1,0:T(8,128)} %pack.1), calls=%async_computation | async-start | bytes 1179648 | tf_op jit(solution)/shard_map/all_to_all | solution.py:412
  9.6 0.0 copy-done
  9.6 5.1 %invert.1 = (f32[256,256]{1,0:T(8,128)S(1)}, bf16[256,256]{1,0:T(8,128)(2,1)S(1)}, bf16[256,256]{1,0:T(8,128)(2,1)S(1)}, f32[1,1]{1,0:T(1,128)}) custom-call(f32[256,256]{1,0:T(8,128)S(1)} %copy-done), custom_call_target="tpu_custom_call" | custom-call | flops 1342177280 | bytes 1048576 | tf_op jit(solution)/shard_map/invert/pallas_call | solution.py:118
  14.7 10.5 %all-to-all-done.received.shared = f32[16,72,128]{2,1,0:T(8,128)S(1)} async-done(((f32[16,72,128]{2,1,0:T(8,128)}), f32[16,72,128]{2,1,0:T(8,128)S(1)}, u32[]{:S(2)}, u32[]{:S(2)}) %all-to-all-start) | async-done | bytes 589856 | tf_op jit(solution)/shard_map/all_to_all | solution.py:412
  25.2 4.2 %solve.1 = f32[16,32,256]{2,1,0:T(8,128)S(1)} custom-call(f32[16,72,128]{2,1,0:T(8,128)S(1)} %all-to-all-done.received.shared, f32[16,72,128]{2,1,0:T(8,128)S(1)} %all-to-all-done.received.shared, f32[1,1]{1,0:T(1,128)} %get-tuple-element.9.error, f32[256,256]{1,0:T(8,128)S(1)} %copy-done, f32[256,256]{1,0:T(8,128)S(1)} %get-tuple-element.10.g, ...), custom_call_target="tpu_custom_call" | custom-call | tf_op jit(solution)/shard_map/solve/pallas_call | solution.py:384
  29.4 18.7 %all_to_all.10 = f32[16,32,256]{2,1,0:T(8,128)S(1)} all-to-all(f32[16,32,256]{2,1,0:T(8,128)S(1)} %solve.1), channel_id=1, replica_groups=mesh['groups'=2,'tm'=16] {'tm'}, dimensions={0} | all-to-all | bytes 1048576 | tf_op jit(solution)/shard_map/all_to_all | solution.py:421
  48.1 1.0 %copy.7 = f32[2,256,256]{2,1,0:T(8,128)} copy(f32[2,256,256]{1,2,0:T(8,128)S(1)} %bitcast.5) | data formatting | bytes 1048576 | tf_op jit(solution)/shard_map/reshape | solution.py:424
  (1 shorter events, 0.0 us)
Async XLA Ops:
  2.1 7.6 %copy-start = (f32[256,256]{1,0:T(8,128)S(1)}, f32[256,256]{1,0:T(8,128)}, u32[]{:S(2)}) copy-start(f32[256,256]{1,0:T(8,128)} %spatial.3) | copy-start | bytes 786436
  2.1 23.1 %all-to-all-start = ((f32[16,72,128]{2,1,0:T(8,128)}), f32[16,72,128]{2,1,0:T(8,128)S(1)}, u32[]{:S(2)}, u32[]{:S(2)}) async-start(f32[16,72,128]{2,1,0:T(8,128)} %pack.1), calls=%async_computation | async-start | bytes 1179648 | tf_op jit(solution)/shard_map/all_to_all | solution.py:412

commit v5 on v3

--- a/solution.py
+++ b/solution.py
@@ -11,11 +11,15 @@
 BF16 = jnp.bfloat16
 SUBLANES = 8
 LANES = 128
+MATRIX_ROWS = 512
+WRITTEN_OUT = 1
+UNCHECKED_STEPS = 2
 TOLERANCE = 1e-5
 STEP_LIMIT = 2000
 COARSE_LIMIT = 14
 FINE_LIMIT = 80
 INVERSE_TOLERANCE = 1e-5
+EASY_STEPS = 6
 CORRECTION_TOLERANCE = 1e-6
 REFINEMENT_LIMIT = 8
 
@@ -39,7 +43,7 @@
 
 
 def loop(count, body, start):
-    if count <= 32:
+    if count <= WRITTEN_OUT:
         carry = start
         for i in range(count):
             carry = body(i, carry)
@@ -124,43 +128,73 @@
     )(spatial)
 
 
-def pack_kernel(rates, right_side, weights, out):
+def tail_rows(per_segment, halves):
+    rows = per_segment * halves + per_segment
+    return rows + -rows % SUBLANES
+
+
+def pack_kernel(rates, right_side, weights, out, turned, source, rate, weight, arrivals, departures):
     steps, size, column_count = right_side.shape
     devices = out.shape[0]
     columns = column_count // devices
     halves = size // LANES
-    tail = steps * halves * columns
+    rows = halves * columns
+    tail = tail_rows(steps, halves)
+    loads = [pltpu.make_async_copy(right_side.at[e], source.at[e], arrivals.at[e]) for e in range(steps)]
+    loads.append(pltpu.make_async_copy(rates, rate, arrivals.at[steps]))
+    loads.append(pltpu.make_async_copy(weights, weight, arrivals.at[steps + 1]))
+    for copy in loads:
+        copy.start()
+    sizes = [rows] * (steps - 1) + [rows + tail]
+    stores = []
     for e in range(steps):
-        turned = right_side[e].T
+        part = pl.ds(e * rows, sizes[e])
+        stores.append(pltpu.make_async_copy(turned.at[:, part, :], out.at[:, part, :], departures.at[e]))
+    for e in range(steps):
+        loads[e].wait()
+        value = source[e].T
         for i in range(devices):
             for k in range(halves):
-                out[i, pl.ds((e * halves + k) * columns, columns), :] = turned[
+                turned[i, pl.ds(e * rows + k * columns, columns), :] = value[
                     i * columns : (i + 1) * columns, k * LANES : (k + 1) * LANES
                 ]
-    row = lax.broadcasted_iota(jnp.int32, (out.shape[1] - tail, LANES), 0)
-    last = jnp.zeros(row.shape, F32)
-    for e in range(steps):
-        for k in range(halves):
-            weight = weights[pl.ds(e, 1), pl.ds(k * LANES, LANES)]
-            last = jnp.where(row == e * halves + k, weight, last)
-        last = jnp.where(row == steps * halves + e, rates[e], last)
-    for i in range(devices):
-        out[i, pl.ds(tail, row.shape[0]), :] = last
+        if e == steps - 1:
+            for copy in loads[steps:]:
+                copy.wait()
+            row = lax.broadcasted_iota(jnp.int32, (tail, LANES), 0)
+            last = jnp.zeros(row.shape, F32)
+            for j in range(steps):
+                for k in range(halves):
+                    piece = weight[pl.ds(j, 1), pl.ds(k * LANES, LANES)]
+                    last = jnp.where(row == j * halves + k, piece, last)
+                last = jnp.where(row == steps * halves + j, rate[j], last)
+            for i in range(devices):
+                turned[i, pl.ds(steps * rows, tail), :] = last
+        stores[e].start()
+    for copy in stores:
+        copy.wait()
 
 
 def pack(persistence, right_side, weights, devices):
     steps, size, column_count = right_side.shape
     halves = size // LANES
-    rows = steps * halves * (column_count // devices)
-    total = rows + steps * halves + steps
-    total += -total % SUBLANES
-    vmem, smem = pl.BlockSpec(memory_space=pltpu.VMEM), pl.BlockSpec(memory_space=pltpu.SMEM)
+    total = steps * halves * (column_count // devices) + tail_rows(steps, halves)
+    anywhere = pl.BlockSpec(memory_space=pl.ANY)
+    shape = (devices, total, LANES)
     return pl.pallas_call(
         pack_kernel,
-        out_shape=jax.ShapeDtypeStruct((devices, total, LANES), F32),
-        in_specs=[smem, vmem, vmem],
-        out_specs=vmem,
-        compiler_params=pltpu.CompilerParams(vmem_limit_bytes=16 * 2**20),
+        out_shape=jax.ShapeDtypeStruct(shape, F32),
+        in_specs=[anywhere] * 3,
+        out_specs=anywhere,
+        scratch_shapes=[
+            pltpu.VMEM(shape, F32),
+            pltpu.VMEM(right_side.shape, F32),
+            pltpu.SMEM(persistence.shape, F32),
+            pltpu.VMEM(weights.shape, F32),
+            pltpu.SemaphoreType.DMA((steps + 2,)),
+            pltpu.SemaphoreType.DMA((steps,)),
+        ],
+        compiler_params=pltpu.CompilerParams(vmem_limit_bytes=56 * 2**20),
         name="pack",
     )(persistence, right_side, weights)
 
@@ -173,7 +207,11 @@
     size = g.shape[0]
     steps = segments * per_segment
     halves = size // LANES
-    tail = per_segment * halves * columns
+    tail = received.shape[1] - tail_rows(per_segment, halves)
+    group = max(MATRIX_ROWS // columns, 1)
+    if steps % group:
+        group = 1
+    groups = steps // group
 
     def rows(start):
         if isinstance(start, int):
@@ -195,6 +233,9 @@
         i, j = source(t)
         return lanes([received[i, rows((j * halves + k) * columns), :] for k in range(halves)])
 
+    def at_step(ref, t):
+        return lanes([ref[pl.ds(t, 1), :]] * halves)
+
     def over_lanes(value):
         return jnp.sum(value, axis=1, keepdims=True)
 
@@ -204,71 +245,100 @@
     def ratio(top, bottom):
         return jnp.where(bottom > 0.0, top / jnp.where(bottom > 0.0, bottom, 1.0), 0.0)
 
-    def factor(t, last):
+    def over_steps(body, start):
+        def over_group(i, carry):
+            for k in range(group):
+                carry = body(i * group + k, carry)
+            return carry
+
+        return loop(groups, over_group, start)
+
+    def over_steps_back(body, start):
+        def over_group(i, carry):
+            for k in reversed(range(group)):
+                carry = body((groups - 1 - i) * group + k, carry)
+            return carry
+
+        return loop(groups, over_group, start)
+
+    def gather(t, carry):
         i, j = source(t)
         w[t] = lanes([received[i, pl.ds(tail + j * halves + k, 1), :] for k in range(halves)])
-        rate = received[i, pl.ds(tail + per_segment * halves + j, 1), :]
-        link = rate * last
-        inverse_pivot = 1.0 / (1.0 + rate * rate - rate * link)
-        rates[t] = lanes([rate] * halves)
-        e[t] = lanes([link] * halves)
-        d[t] = lanes([inverse_pivot] * halves)
-        return inverse_pivot
-
-    loop(steps, factor, jnp.zeros((1, LANES), F32))
-
-    biggest = loop(steps, lambda t, acc: jnp.maximum(acc, jnp.abs(right_side(t))), zero())
+        rates[pl.ds(t, 1), :] = received[i, pl.ds(tail + per_segment * halves + j, 1), :]
+        return carry
+
+    over_steps(gather, 0)
+    e[...] = 1.0 / (rates[...] * rates[...])
+
+    def pivot(t, last):
+        value = e[pl.ds(t, 1), :] * (last + 1.0)
+        d[pl.ds(t, 1), :] = value
+        return value
+
+    over_steps(pivot, jnp.zeros((1, LANES), F32))
+    pivots = d[...] / (d[...] + 1.0)
+    d[...] = pivots
+    first_step = lax.broadcasted_iota(jnp.int32, pivots.shape, 0) == 0
+    e[...] = rates[...] * jnp.where(first_step, 0.0, pltpu.roll(pivots, 1, 0))
+
+    biggest = over_steps(lambda t, acc: jnp.maximum(acc, jnp.abs(right_side(t))), zero())
     biggest = jnp.max(biggest, axis=1, keepdims=True)
     biggest = jnp.where(biggest > 0.0, biggest, 1.0)
     shrink = 1.0 / biggest
 
-    def load(t, carry):
-        r[at(t), :] = right_side(t) * shrink
-        return carry
-
-    loop(steps, load, 0)
-
-    def down(t, last):
-        value = z[at(t), :] + e[t] * last
-        z[at(t), :] = value
-        return value
-
     def start(first):
-        z[...] = exact_dot(r[...], g[...])
-        loop(steps, down, zero())
-
-        def up(k, carry):
+        def down(i, last):
+            ts = [i * group + k for k in range(group)]
+            value = jnp.concatenate([right_side(t) if first else r[at(t), :] for t in ts], axis=0)
+            value = exact_dot(value, g[...])
+            for k, t in enumerate(ts):
+                piece = value[k * columns : (k + 1) * columns]
+                if first:
+                    piece = piece * shrink
+                last = piece + at_step(e, t) * last
+                z[at(t), :] = last
+            return last
+
+        loop(groups, down, zero())
+
+        def up(t, carry):
             above, acc = carry
-            t = steps - 1 - k
-            value = z[at(t), :] * d[t] + above
+            value = z[at(t), :] * at_step(d, t) + above
             x[at(t), :] = value if first else x[at(t), :] + value
             r[at(t), :] = value
             p[at(t), :] = value
-            return e[t] * value, acc + w[t] * value * value
-
-        unused, acc = loop(steps, up, (zero(), zero()))
+            return at_step(e, t) * value, acc + w[t] * value * value
+
+        unused, acc = over_steps_back(up, (zero(), zero()))
         return over_lanes(acc)
 
-    def weigh(t, carry):
-        z[at(t), :] = w[t] * p[at(t), :]
-        return carry
-
     def step(state):
-        count, square, limit, unused = state
-        loop(steps, weigh, 0)
-        z[...] = split_dot(z[...], g_high[...], g_low[...])
-        loop(steps, down, zero())
-
-        def up(k, carry):
+        square, beta = state
+
+        def down(i, last):
+            ts = [i * group + k for k in range(group)]
+            pieces = []
+            for t in ts:
+                direction = r[at(t), :] + beta * p[at(t), :]
+                p[at(t), :] = direction
+                pieces.append(w[t] * direction)
+            value = split_dot(jnp.concatenate(pieces, axis=0), g_high[...], g_low[...])
+            for k, t in enumerate(ts):
+                last = value[k * columns : (k + 1) * columns] + at_step(e, t) * last
+                z[at(t), :] = last
+            return last
+
+        loop(groups, down, zero())
+
+        def up(t, carry):
             above, own, cross = carry
-            t = steps - 1 - k
-            value = z[at(t), :] * d[t] + above
+            value = z[at(t), :] * at_step(d, t) + above
             z[at(t), :] = value
             direction = p[at(t), :]
             weighted = w[t] * direction
-            return e[t] * value, own + weighted * direction, cross + weighted * value
-
-        unused, own, cross = loop(steps, up, (zero(), zero(), zero()))
+            return at_step(e, t) * value, own + weighted * direction, cross + weighted * value
+
+        unused, own, cross = over_steps_back(up, (zero(), zero(), zero()))
         own, cross = over_lanes(own), over_lanes(cross)
         alpha = ratio(square, own + cross)
 
@@ -279,26 +349,29 @@
             r[at(t), :] = value
             return acc + w[t] * value * value
 
-        new_square = over_lanes(loop(steps, advance, zero()))
-        beta = ratio(new_square, square)
-
-        def turn(t, carry):
-            p[at(t), :] = r[at(t), :] + beta * p[at(t), :]
-            return carry
-
-        loop(steps, turn, 0)
+        new_square = over_lanes(over_steps(advance, zero()))
         share = ratio(cross, own + cross)
-        return count + 1, new_square, limit, jnp.max(share * share * new_square - limit)
-
-    def goes_on(state):
-        count, unused, unused_limit, excess = state
-        return jnp.logical_and(count < STEP_LIMIT, excess > 0.0)
+        return new_square, ratio(new_square, square), share * share * new_square
 
     def iterate(square):
-        lax.while_loop(goes_on, step, (0, square, square * TOLERANCE**2, jnp.max(square)))
+        limit = square * TOLERANCE**2
+        state = lax.fori_loop(
+            0, UNCHECKED_STEPS, lambda i, state: step(state)[:2], (square, jnp.zeros_like(square))
+        )
+
+        def goes_on(state):
+            count, unused, unused_beta, excess = state
+            return jnp.logical_and(count < STEP_LIMIT, excess > 0.0)
+
+        def checked(state):
+            count, square, beta, unused = state
+            square, beta, left = step((square, beta))
+            return count + 1, square, beta, jnp.max(left - limit)
+
+        return lax.while_loop(goes_on, checked, (UNCHECKED_STEPS, *state, F32(1.0)))[0]
 
     whole_square = start(True)
-    iterate(whole_square)
+    count = iterate(whole_square)
 
     def refine(state):
         count, unused = state
@@ -306,16 +379,15 @@
         def combine(t, last):
             here = x[at(t), :]
             after = jnp.minimum(t + 1, steps - 1)
-            link = jnp.where(t + 1 < steps, 1.0, 0.0) * rates[after]
-            value = (1.0 + rates[t] * rates[t]) * here - rates[t] * last - link * x[at(after), :]
-            z[at(t), :] = value
+            link = jnp.where(t + 1 < steps, 1.0, 0.0) * at_step(rates, after)
+            rate = at_step(rates, t)
+            z[at(t), :] = (1.0 + rate * rate) * here - rate * last - link * x[at(after), :]
             return here
 
         lax.fori_loop(0, steps, combine, zero())
         z[...] = exact_dot(z[...], spatial[...])
 
         def subtract(t, carry):
-            i, j = source(t)
             r[at(t), :] = right_side(t) * shrink - z[at(t), :] - w[t] * x[at(t), :]
             return carry
 
@@ -328,21 +400,22 @@
         count, excess = state
         return jnp.logical_and(count < REFINEMENT_LIMIT, excess > 0.0)
 
-    lax.while_loop(refines, refine, (0, error[0, 0] - INVERSE_TOLERANCE**2))
+    needed = jnp.logical_or(error[0, 0] > INVERSE_TOLERANCE**2, count > EASY_STEPS)
+    lax.while_loop(refines, refine, (0, jnp.where(needed, 1.0, 0.0)))
 
     def store(t, carry):
         i, j = source(t)
         out[i, rows(j * columns), :] = x[at(t), :] * biggest
         return carry
 
-    loop(steps, store, 0)
+    over_steps(store, 0)
 
 
 def solve(received, spatial, inverse, segments, per_segment, columns):
     size = spatial.shape[0]
     steps = segments * per_segment
     state = pltpu.VMEM((steps * columns, size), F32)
-    per_step = pltpu.VMEM((steps, 1, size), F32)
+    per_step = pltpu.VMEM((steps, LANES), F32)
     full, high, low, error = inverse
     vmem, smem = pl.BlockSpec(memory_space=pltpu.VMEM), pl.BlockSpec(memory_space=pltpu.SMEM)
     return pl.pallas_call(
@@ -350,7 +423,7 @@
         out_shape=jax.ShapeDtypeStruct((segments, per_segment * columns, size), F32),
         in_specs=[vmem, smem, vmem, vmem, vmem, vmem],
         out_specs=vmem,
-        scratch_shapes=[state] * 4 + [per_step] * 4,
+        scratch_shapes=[state] * 4 + [pltpu.VMEM((steps, 1, size), F32)] + [per_step] * 3,
         compiler_params=pltpu.CompilerParams(vmem_limit_bytes=40 * 2**20),
         name="solve",
     )(received, error, spatial, full, high, low)

time: 51.3 us -> 49 us (0.955)
  local copies, waits for them, and re-layouts: 3.41 us -> 1.04 us
    unnamed x8 -> x2, local copies, waits for them, and re-layouts: 2.38 us -> 0.01 us
where the time goes in v5:
time: 49 us; the launch traced here: 48.7 us
  blocking collectives  18.7 us (38%)
  Pallas kernels  11 us (22%)
  waiting for transfers between devices  10.5 us (21%)
  starting transfers between devices  7.53 us (15%)
  local copies, waits for them, and re-layouts  1.04 us (2%)
    all_to_all x1, blocking collectives, body(): returned = lax.all_to_all(solved, 'tm', 0, 0, tiled=True)  18.7 us
    all_to_all x1, waiting for transfers between devices, body(): received = lax.all_to_all(packed, 'tm', 0, 0, tiled=True)  10.5 us
    all_to_all x1, starting transfers between devices, body(): received = lax.all_to_all(packed, 'tm', 0, 0, tiled=True)  7.53 us
    pallas_call x1, Pallas kernels, invert_spatial(): pl.pallas_call(invert_kernel, out_shape=[full, half, half, jax.ShapeDtype...  5.06 us
    pallas_call x1, Pallas kernels, solve(): pl.pallas_call(functools.partial(solve_kernel, segments, per_segment, col...  3.87 us
    pallas_call x1, Pallas kernels, pack(): pl.pallas_call(pack_kernel, out_shape=jax.ShapeDtypeStruct(shape, F32), i...  2.04 us
    reshape x1, local copies, waits for them, and re-layouts, body(): jnp.transpose(returned, (1, 3, 0, 2))  1 us
  transfers between devices with their start and end apart: 1, of which 1 were waited for; matrix products, arithmetic and copies ran while one was open for 0% of the time, Pallas kernels for 10%

profile of v5, /device:TPU:0, one launch (start us, length us, event | category | flops | bytes accessed | tf_op | source)
XLA Modules:
  0.0 48.7 jit_solution(13314837673871409371)
XLA Ops:
  0.0 2.0 %pack.1 = f32[16,72,128]{2,1,0:T(8,128)} custom-call(f32[2]{0:T(128)} %rates.1, f32[2,256,256]{2,1,0:T(8,128)} %right_side.1, f32[2,256]{1,0:T(2,128)} %weights.1), custom_call_target="tpu_custom_call" | custom-call | tf_op jit(solution)/shard_map/pack/pallas_call | solution.py:184
  2.0 0.0 copy-start
  2.1 7.5 %all-to-all-start = ((f32[16,72,128]{2,1,0:T(8,128)}), f32[16,72,128]{2,1,0:T(8,128)S(1)}, u32[]{:S(2)}, u32[]{:S(2)}) async-start(f32[16,72,128]{2,1,0:T(8,128)} %pack.1), calls=%async_computation | async-start | bytes 1179648 | tf_op jit(solution)/shard_map/all_to_all | solution.py:447
  9.6 0.0 copy-done
  9.6 5.1 %invert.1 = (f32[256,256]{1,0:T(8,128)S(1)}, bf16[256,256]{1,0:T(8,128)(2,1)S(1)}, bf16[256,256]{1,0:T(8,128)(2,1)S(1)}, f32[1,1]{1,0:T(1,128)}) custom-call(f32[256,256]{1,0:T(8,128)S(1)} %copy-done), custom_call_target="tpu_custom_call" | custom-call | flops 1342177280 | bytes 1048576 | tf_op jit(solution)/shard_map/invert/pallas_call | solution.py:120
  14.7 10.5 %all-to-all-done.received = f32[16,72,128]{2,1,0:T(8,128)S(1)} async-done(((f32[16,72,128]{2,1,0:T(8,128)}), f32[16,72,128]{2,1,0:T(8,128)S(1)}, u32[]{:S(2)}, u32[]{:S(2)}) %all-to-all-start) | async-done | bytes 589856 | tf_op jit(solution)/shard_map/all_to_all | solution.py:447
  25.1 3.9 %solve.1 = f32[16,32,256]{2,1,0:T(8,128)S(1)} custom-call(f32[16,72,128]{2,1,0:T(8,128)S(1)} %all-to-all-done.received, f32[1,1]{1,0:T(1,128)} %get-tuple-element.9.error, f32[256,256]{1,0:T(8,128)S(1)} %copy-done, f32[256,256]{1,0:T(8,128)S(1)} %get-tuple-element.10.g, bf16[256,256]{1,0:T(8,128)(2,1)S(1)} %get-tuple-element.11.g_high, ...), custom_call_target="tpu_custom_call" | custom-call | tf_op jit(solution)/shard_map/solve/pallas_call | solution.py:421
  29.0 18.7 %all_to_all.10 = f32[16,32,256]{2,1,0:T(8,128)S(1)} all-to-all(f32[16,32,256]{2,1,0:T(8,128)S(1)} %solve.1), channel_id=1, replica_groups=mesh['groups'=2,'tm'=16] {'tm'}, dimensions={0} | all-to-all | bytes 1048576 | tf_op jit(solution)/shard_map/all_to_all | solution.py:454
  47.8 1.0 %copy.7 = f32[2,256,256]{2,1,0:T(8,128)} copy(f32[2,256,256]{1,2,0:T(8,128)S(1)} %bitcast.5) | data formatting | bytes 1048576 | tf_op jit(solution)/shard_map/reshape | solution.py:456
  (1 shorter events, 0.0 us)
Async XLA Ops:
  2.0 7.6 %copy-start = (f32[256,256]{1,0:T(8,128)S(1)}, f32[256,256]{1,0:T(8,128)}, u32[]{:S(2)}) copy-start(f32[256,256]{1,0:T(8,128)} %spatial.3) | copy-start | bytes 786436
  2.1 23.1 %all-to-all-start = ((f32[16,72,128]{2,1,0:T(8,128)}), f32[16,72,128]{2,1,0:T(8,128)S(1)}, u32[]{:S(2)}, u32[]{:S(2)}) async-start(f32[16,72,128]{2,1,0:T(8,128)} %pack.1), calls=%async_computation | async-start | bytes 1179648 | tf_op jit(solution)/shard_map/all_to_all | solution.py:447

commit v6 on v5

--- a/solution.py
+++ b/solution.py
@@ -312,9 +312,7 @@
         unused, acc = over_steps_back(up, (zero(), zero()))
         return over_lanes(acc)
 
-    def step(state):
-        square, beta = state
-
+    def turn(square, beta):
         def down(i, last):
             ts = [i * group + k for k in range(group)]
             pieces = []
@@ -331,47 +329,70 @@
         loop(groups, down, zero())
 
         def up(t, carry):
-            above, own, cross = carry
+            above, own, cross, image = carry
             value = z[at(t), :] * at_step(d, t) + above
             z[at(t), :] = value
             direction = p[at(t), :]
             weighted = w[t] * direction
-            return at_step(e, t) * value, own + weighted * direction, cross + weighted * value
-
-        unused, own, cross = over_steps_back(up, (zero(), zero(), zero()))
-        own, cross = over_lanes(own), over_lanes(cross)
+            both = w[t] * value
+            own, cross, image = own + weighted * direction, cross + weighted * value, image + both * value
+            return at_step(e, t) * value, own, cross, image
+
+        unused, own, cross, image = over_steps_back(up, (zero(), zero(), zero(), zero()))
+        own, cross, image = over_lanes(own), over_lanes(cross), over_lanes(image)
         alpha = ratio(square, own + cross)
-
-        def advance(t, acc):
+        after = jnp.maximum(alpha * alpha * (own + 2.0 * cross + image) - square, 0.0)
+        share = ratio(cross, own + cross)
+        return alpha, share * share * after
+
+    def advance(square, alpha):
+        def move(t, acc):
             change = z[at(t), :]
             x[at(t), :] -= alpha * change
             value = r[at(t), :] - alpha * (p[at(t), :] + change)
             r[at(t), :] = value
             return acc + w[t] * value * value
 
-        new_square = over_lanes(over_steps(advance, zero()))
-        share = ratio(cross, own + cross)
-        return new_square, ratio(new_square, square), share * share * new_square
+        new_square = over_lanes(over_steps(move, zero()))
+        return new_square, ratio(new_square, square)
 
     def iterate(square):
         limit = square * TOLERANCE**2
-        state = lax.fori_loop(
-            0, UNCHECKED_STEPS, lambda i, state: step(state)[:2], (square, jnp.zeros_like(square))
-        )
+
+        def unchecked(i, state):
+            square, beta = state
+            return advance(square, turn(square, beta)[0])
+
+        square, beta = lax.fori_loop(0, UNCHECKED_STEPS, unchecked, (square, jnp.zeros_like(square)))
 
         def goes_on(state):
-            count, unused, unused_beta, excess = state
+            count, unused, unused_beta, unused_alpha, excess = state
             return jnp.logical_and(count < STEP_LIMIT, excess > 0.0)
 
         def checked(state):
-            count, square, beta, unused = state
-            square, beta, left = step((square, beta))
-            return count + 1, square, beta, jnp.max(left - limit)
-
-        return lax.while_loop(goes_on, checked, (UNCHECKED_STEPS, *state, F32(1.0)))[0]
+            count, square, beta, alpha, unused = state
+            alpha, left = turn(square, beta)
+            excess = jnp.max(left - limit)
+
+            def more():
+                return advance(square, alpha)
+
+            square, beta = lax.cond(excess > 0.0, more, lambda: (square, beta))
+            return count + 1, square, beta, jnp.where(excess > 0.0, 0.0, alpha), excess
+
+        state = (UNCHECKED_STEPS, square, beta, jnp.zeros_like(square), F32(1.0))
+        state = lax.while_loop(goes_on, checked, state)
+        return state[0], state[3]
+
+    def finish(alpha):
+        def move(t, carry):
+            x[at(t), :] -= alpha * z[at(t), :]
+            return carry
+
+        lax.fori_loop(0, steps, move, 0)
 
     whole_square = start(True)
-    count = iterate(whole_square)
+    count, alpha = iterate(whole_square)
 
     def refine(state):
         count, unused = state
@@ -393,7 +414,7 @@
 
         lax.fori_loop(0, steps, subtract, 0)
         square = start(False)
-        iterate(square)
+        finish(iterate(square)[1])
         return count + 1, jnp.max(square - whole_square * CORRECTION_TOLERANCE**2)
 
     def refines(state):
@@ -401,14 +422,25 @@
         return jnp.logical_and(count < REFINEMENT_LIMIT, excess > 0.0)
 
     needed = jnp.logical_or(error[0, 0] > INVERSE_TOLERANCE**2, count > EASY_STEPS)
-    lax.while_loop(refines, refine, (0, jnp.where(needed, 1.0, 0.0)))
 
     def store(t, carry):
         i, j = source(t)
-        out[i, rows(j * columns), :] = x[at(t), :] * biggest
+        out[i, rows(j * columns), :] = (x[at(t), :] - alpha * z[at(t), :]) * biggest
         return carry
 
     over_steps(store, 0)
+
+    @pl.when(needed)
+    def refined():
+        finish(alpha)
+        lax.while_loop(refines, refine, (0, F32(1.0)))
+
+        def store_refined(t, carry):
+            i, j = source(t)
+            out[i, rows(j * columns), :] = x[at(t), :] * biggest
+            return carry
+
+        lax.fori_loop(0, steps, store_refined, 0)
 
 
 def solve(received, spatial, inverse, segments, per_segment, columns):
@@ -429,6 +461,41 @@
     )(received, error, spatial, full, high, low)
 
 
+def unpack_kernel(returned, out, turned, departures):
+    steps, size, column_count = out.shape
+    devices = returned.shape[0]
+    columns = column_count // devices
+    spans = column_count // LANES
+    per_span = devices // spans
+    stores = []
+    for e in range(steps):
+        for k in range(spans):
+            pieces = [returned[k * per_span + i, pl.ds(e * columns, columns), :] for i in range(per_span)]
+            turned[e, k] = jnp.concatenate(pieces, axis=0).T
+            some = out.at[e, :, pl.ds(k * LANES, LANES)]
+            stores.append(pltpu.make_async_copy(turned.at[e, k], some, departures.at[e * spans + k]))
+            stores[-1].start()
+    for copy in stores:
+        copy.wait()
+
+
+def unpack(returned, steps, column_count):
+    size = returned.shape[2]
+    spans = column_count // LANES
+    return pl.pallas_call(
+        unpack_kernel,
+        out_shape=jax.ShapeDtypeStruct((steps, size, column_count), F32),
+        in_specs=[pl.BlockSpec(memory_space=pltpu.VMEM)],
+        out_specs=pl.BlockSpec(memory_space=pl.ANY),
+        scratch_shapes=[
+            pltpu.VMEM((steps, spans, size, LANES), F32),
+            pltpu.SemaphoreType.DMA((steps * spans,)),
+        ],
+        compiler_params=pltpu.CompilerParams(vmem_limit_bytes=16 * 2**20),
+        name="unpack",
+    )(returned)
+
+
 def pad_columns(received, per_segment, halves, columns, padded):
     devices, total, width = received.shape
     rows = per_segment * halves * columns
@@ -452,6 +519,8 @@
         solved = solved.reshape(devices, per_segment, padded, size)[:, :, :columns]
         solved = solved.reshape(devices, per_segment * columns, size)
     returned = lax.all_to_all(solved, "tm", 0, 0, tiled=True)
+    if columns % SUBLANES == 0:
+        return unpack(returned, per_segment, column_count)
     returned = returned.reshape(devices, per_segment, columns, size)
     return jnp.transpose(returned, (1, 3, 0, 2)).reshape(per_segment, size, column_count)
 

time: 49 us -> 48.8 us (level)
  local copies, waits for them, and re-layouts: 1.04 us -> 0.01 us
  Pallas kernels: 11 us -> 11.7 us
    reshape x2 -> x0, local copies, waits for them, and re-layouts: 1.03 us -> none  [the longest x1 1 us: body(): jnp.transpose(returned, (1, 3, 0, 2))]
    pallas_call x0 -> x1, Pallas kernels: none -> 0.92 us  [unpack(): pl.pallas_call(unpack_kernel, out_shape=jax.ShapeDtypeStruct((steps, size...]
where the time goes in v6:
time: 48.8 us; the launch traced here: 48.5 us
  blocking collectives  18.7 us (38%)
  Pallas kernels  11.7 us (24%)
  waiting for transfers between devices  10.5 us (22%)
  starting transfers between devices  7.53 us (15%)
    all_to_all x1, blocking collectives, body(): returned = lax.all_to_all(solved, 'tm', 0, 0, tiled=True)  18.7 us
    all_to_all x1, waiting for transfers between devices, body(): received = lax.all_to_all(packed, 'tm', 0, 0, tiled=True)  10.5 us
    all_to_all x1, starting transfers between devices, body(): received = lax.all_to_all(packed, 'tm', 0, 0, tiled=True)  7.53 us
    pallas_call x1, Pallas kernels, invert_spatial(): pl.pallas_call(invert_kernel, out_shape=[full, half, half, jax.ShapeDtype...  5.06 us
    pallas_call x1, Pallas kernels, solve(): pl.pallas_call(functools.partial(solve_kernel, segments, per_segment, col...  3.73 us
    pallas_call x1, Pallas kernels, pack(): pl.pallas_call(pack_kernel, out_shape=jax.ShapeDtypeStruct(shape, F32), i...  2.04 us
  transfers between devices with their start and end apart: 1, of which 1 were waited for; matrix products, arithmetic and copies ran while one was open for 0% of the time, Pallas kernels for 10%

profile of v6, /device:TPU:0, one launch (start us, length us, event | category | flops | bytes accessed | tf_op | source)
XLA Modules:
  0.0 48.5 jit_solution(16365173732145992264)
XLA Ops:
  0.0 2.0 %pack.1 = f32[16,72,128]{2,1,0:T(8,128)} custom-call(f32[2]{0:T(128)} %rates.1, f32[2,256,256]{2,1,0:T(8,128)} %right_side.1, f32[2,256]{1,0:T(2,128)} %weights.1), custom_call_target="tpu_custom_call" | custom-call | tf_op jit(solution)/shard_map/pack/pallas_call | solution.py:184
  2.0 0.0 copy-start
  2.1 7.5 %all-to-all-start = ((f32[16,72,128]{2,1,0:T(8,128)}), f32[16,72,128]{2,1,0:T(8,128)S(1)}, u32[]{:S(2)}, u32[]{:S(2)}) async-start(f32[16,72,128]{2,1,0:T(8,128)} %pack.1), calls=%async_computation | async-start | bytes 1179648 | tf_op jit(solution)/shard_map/all_to_all | solution.py:514
  9.6 0.0 copy-done
  9.6 5.1 %invert.1 = (f32[256,256]{1,0:T(8,128)S(1)}, bf16[256,256]{1,0:T(8,128)(2,1)S(1)}, bf16[256,256]{1,0:T(8,128)(2,1)S(1)}, f32[1,1]{1,0:T(1,128)}) custom-call(f32[256,256]{1,0:T(8,128)S(1)} %copy-done), custom_call_target="tpu_custom_call" | custom-call | flops 1342177280 | bytes 1048576 | tf_op jit(solution)/shard_map/invert/pallas_call | solution.py:120
  14.7 10.5 %all-to-all-done.received = f32[16,72,128]{2,1,0:T(8,128)S(1)} async-done(((f32[16,72,128]{2,1,0:T(8,128)}), f32[16,72,128]{2,1,0:T(8,128)S(1)}, u32[]{:S(2)}, u32[]{:S(2)}) %all-to-all-start) | async-done | bytes 589856 | tf_op jit(solution)/shard_map/all_to_all | solution.py:514
  25.1 3.7 %solve.1 = f32[16,32,256]{2,1,0:T(8,128)S(1)} custom-call(f32[16,72,128]{2,1,0:T(8,128)S(1)} %all-to-all-done.received, f32[1,1]{1,0:T(1,128)} %get-tuple-element.9.error, f32[256,256]{1,0:T(8,128)S(1)} %copy-done, f32[256,256]{1,0:T(8,128)S(1)} %get-tuple-element.10.g, bf16[256,256]{1,0:T(8,128)(2,1)S(1)} %get-tuple-element.11.g_high, ...), custom_call_target="tpu_custom_call" | custom-call | tf_op jit(solution)/shard_map/solve/pallas_call | solution.py:453
  28.9 18.7 %all_to_all.10.returned = f32[16,32,256]{2,1,0:T(8,128)S(1)} all-to-all(f32[16,32,256]{2,1,0:T(8,128)S(1)} %solve.1), channel_id=1, replica_groups=mesh['groups'=2,'tm'=16] {'tm'}, dimensions={0} | all-to-all | bytes 1048576 | tf_op jit(solution)/shard_map/all_to_all | solution.py:521
  47.6 0.9 %unpack.1 = f32[2,256,256]{2,1,0:T(8,128)} custom-call(f32[16,32,256]{2,1,0:T(8,128)S(1)} %all_to_all.10.returned), custom_call_target="tpu_custom_call" | custom-call | tf_op jit(solution)/shard_map/unpack/pallas_call | solution.py:485
Async XLA Ops:
  2.0 7.6 %copy-start = (f32[256,256]{1,0:T(8,128)S(1)}, f32[256,256]{1,0:T(8,128)}, u32[]{:S(2)}) copy-start(f32[256,256]{1,0:T(8,128)} %spatial.3) | copy-start | bytes 786436
  2.1 23.1 %all-to-all-start = ((f32[16,72,128]{2,1,0:T(8,128)}), f32[16,72,128]{2,1,0:T(8,128)S(1)}, u32[]{:S(2)}, u32[]{:S(2)}) async-start(f32[16,72,128]{2,1,0:T(8,128)} %pack.1), calls=%async_computation | async-start | bytes 1179648 | tf_op jit(solution)/shard_map/all_to_all | solution.py:514
